TPU v7x, 128 devices: a whole 4x4x4 slice. The times are simulated.
128 devices in a mesh: seq: 16 (over z, y_hi, core), head: 8 (over y_lo, x).
Axes of the slice: x: 4, y: 4 (y_hi: 2, y_lo: 2; y = y_hi * 2 + y_lo), z: 4, core: 2. Of those that a mesh axis runs over, the one named last changes fastest.
Arguments:
- queries: bfloat16 [8192, 8192], P('seq', 'head'), may hold values from -7 to 7
- key_states: bfloat16 [8192, 1024], P(('seq', 'head')), may hold values from -6 to 6
- value_states: bfloat16 [8192, 1024], P(('seq', 'head')), may hold values from -6 to 6
- passing_rows: int32 [8, 4096], P('head', 'seq'), may hold values from 0 to 511, as said below
Outputs:
- attended: bfloat16 [8192, 8192], P('seq', 'head')
Inputs may be any that keep to these rules, and one draw needn't show every extreme that they name: `passing_rows`: for each KV head and each block the 256 entries are distinct, in increasing order, and include 0 and 511.
All inputs are finite; a program needn't handle non-finite values.
Results may differ from a plain program's by a relative error of at most 0.009.
Values may be sent and summed in bfloat16 or wider, within the bound.
No kernel may reach another device: no remote copies, remote signals or barrier semaphores. Data moves between devices by JAX's collectives and lax.ppermute only.
A program may use at most 320 MiB of HBM per device.

v0:
```python
import jax
import jax.numpy as jnp
from jax import lax
from jax.sharding import PartitionSpec as P

ANCHOR = 256


def spread(block, axis, source):
    block = jnp.where(lax.axis_index(axis) == source, block, jnp.zeros_like(block))
    return lax.psum(block, axis)


def refresh(running, block_queries, block_keys, block_values, usable, score_scale):
    maxima, totals, accumulated = running
    scores = (
        jnp.einsum("tkrd,ckd->ktrc", block_queries, block_keys, preferred_element_type=jnp.float32)
        * score_scale
    )
    masked = jnp.where(usable, scores, -1e30)
    fresh = jnp.maximum(maxima, jnp.max(masked, axis=-1))
    rescale = jnp.exp(maxima - fresh)
    exps = jnp.where(usable, jnp.exp(masked - fresh[..., None]), 0.0)
    totals = totals * rescale + jnp.sum(exps, axis=-1)
    weights = exps.astype(jnp.bfloat16)
    accumulated = accumulated * rescale[..., None] + jnp.einsum(
        "ktrc,ckd->ktrd", weights, block_values, preferred_element_type=jnp.float32
    )
    return (fresh, totals, accumulated)


def over_queries(running, query_grid, key_rows, value_rows, usable_fn, causal, score_scale):
    row_count = query_grid.shape[0]
    block_size = min(row_count, 128)
    results = []
    for offset in range(0, row_count, block_size):
        part_state = tuple((member[:, offset : offset + block_size] for member in running))
        if causal:
            limit = offset + block_size
        else:
            limit = key_rows.shape[0]
        usable = usable_fn(offset, block_size, limit)
        results.append(
            refresh(
                part_state,
                query_grid[offset : offset + block_size],
                key_rows[:limit],
                value_rows[:limit],
                usable,
                score_scale,
            )
        )
    return tuple(
        (
            jnp.concatenate([result_part[member_id] for result_part in results], axis=1)
            for member_id in range(3)
        )
    )


def local(queries, key_states, value_states, passing_rows):
    host_id = lax.axis_index("seq")
    local_keys, local_values = (
        lax.all_to_all(key_states, "head", split_axis=1, concat_axis=0, tiled=True),
        lax.all_to_all(value_states, "head", split_axis=1, concat_axis=0, tiled=True),
    )
    heads_here = passing_rows.shape[0]
    pass_count = passing_rows.shape[1]
    row_count = local_keys.shape[0]
    head_size = local_keys.shape[1] // heads_here
    group_size = queries.shape[1] // (heads_here * head_size)
    score_scale = head_size ** (-0.5)
    key_grid = local_keys.reshape(row_count, heads_here, head_size)
    value_grid = local_values.reshape(row_count, heads_here, head_size)
    query_grid = queries.reshape(row_count, heads_here, group_size, head_size)
    selector = (
        passing_rows[:, :, None] == jnp.arange(row_count, dtype=jnp.int32)[None, None, :]
    ).astype(jnp.bfloat16)
    stacked = jnp.concatenate([key_grid, value_grid], axis=2)
    picked = jnp.einsum(
        "kpr,rkd->pkd", selector, stacked, preferred_element_type=jnp.float32
    ).astype(jnp.bfloat16)
    pass_keys = picked[:, :, :head_size]
    pass_values = picked[:, :, head_size:]
    running = (
        jnp.full((heads_here, row_count, group_size), -1e30, jnp.float32),
        jnp.zeros((heads_here, row_count, group_size), jnp.float32),
        jnp.zeros((heads_here, row_count, group_size, head_size), jnp.float32),
    )

    def causal_mask(offset, block_size, limit):
        return (offset + jnp.arange(block_size)[:, None] >= jnp.arange(limit)[None, :])[:, None, :]

    running = over_queries(
        running, query_grid, key_grid, value_grid, causal_mask, True, score_scale
    )
    anchor_keys, anchor_values = (
        spread(key_grid[:ANCHOR], "seq", 0),
        spread(value_grid[:ANCHOR], "seq", 0),
    )

    def anchor_mask(offset, block_size, limit):
        return jnp.broadcast_to(host_id >= 1, (1, 1, limit))

    running = over_queries(
        running, query_grid, anchor_keys, anchor_values, anchor_mask, False, score_scale
    )
    row_width = pass_keys.shape[0]
    gathered_keys, gathered_values = (
        lax.all_gather(pass_keys, "seq", axis=0, tiled=True),
        lax.all_gather(pass_values, "seq", axis=0, tiled=True),
    )
    row_ids = jnp.arange(gathered_keys.shape[0])
    owner_host = row_ids // row_width
    within = row_ids % row_width
    usable_rows = jnp.where(
        within < pass_count, owner_host < host_id, (owner_host == 0) & (host_id >= 1)
    )[None, None, :]

    def passing_mask(offset, block_size, limit):
        return usable_rows

    running = over_queries(
        running, query_grid, gathered_keys, gathered_values, passing_mask, False, score_scale
    )
    maxima, totals, accumulated = running
    attended = accumulated / totals[..., None]
    return (
        jnp.transpose(attended, (1, 0, 2, 3))
        .reshape(row_count, heads_here * group_size * head_size)
        .astype(jnp.bfloat16)
    )


def solution(mesh):
    in_specs = (
        P("seq", "head"),
        P(("seq", "head"), None),
        P(("seq", "head"), None),
        P("head", "seq"),
    )
    out_specs = P("seq", "head")
    return jax.shard_map(local, mesh=mesh, in_specs=in_specs, out_specs=out_specs, check_vma=False)
```

profile of v0, /device:TPU:113, one launch (start us, length us, event | category | flops | bytes accessed | tf_op | source)
XLA Modules:
  0.0 367.0 jit_solution(14451961918669543510)
XLA Ops:
  6.5 0.9 copy-done
  7.4 0.7 copy_bitcast_fusion
  8.1 4.7 %all-to-all-start.1 = ((bf16[64,8,128]{2,0,1:T(8,128)(2,1)}), bf16[64,8,128]{2,0,1:T(8,128)(2,1)S(1)}, u32[]{:S(2)}, u32[]{:S(2)}) async-start(bf16[64,8,128]{2,0,1:T(8,128)(2,1)} %copy_bitcast_fusion), calls=%async_computation.1 | async-start | bytes 262144 | tf_op jit(solution)/shard_map/all_to_all | solution.py:65
  12.9 1.6 copy_bitcast_fusion.1
  14.4 3.9 %all-to-all-done.1 = bf16[64,8,128]{2,0,1:T(8,128)(2,1)S(1)} async-done(((bf16[64,8,128]{2,0,1:T(8,128)(2,1)}), bf16[64,8,128]{2,0,1:T(8,128)(2,1)S(1)}, u32[]{:S(2)}, u32[]{:S(2)}) %all-to-all-start.1) | async-done | bytes 131104 | tf_op jit(solution)/shard_map/all_to_all | solution.py:65
  18.3 3.4 all-to-all-start
  21.7 0.6 fusion.205
  22.4 0.7 copy.184
  23.1 4.0 %all-to-all-done = bf16[64,8,128]{2,0,1:T(8,128)(2,1)S(1)} async-done(((bf16[64,8,128]{2,0,1:T(8,128)(2,1)}), bf16[64,8,128]{2,0,1:T(8,128)(2,1)S(1)}, u32[]{:S(2)}, u32[]{:S(2)}) %all-to-all-start) | async-done | bytes 131104 | tf_op jit(solution)/shard_map/all_to_all | solution.py:64
  27.1 0.6 fusion.207
  27.8 1.0 fusion.62
  28.9 0.7 fusion.206
  29.6 1.3 fusion.204
  30.9 0.2 copy.259
  31.1 0.2 copy.262
  31.3 0.2 copy.261
  31.4 0.2 copy.260
  31.7 0.7 fusion.143
  32.6 0.6 slice.69
  33.3 0.7 slice.75
  33.9 0.8 fusion.209
  34.8 1.9 fusion.211
  36.6 1.1 fusion.212
  37.8 2.4 fusion.33
  40.2 126.6 %all-reduce.3.cloned.1.call-done = (bf16[256,128]{1,0:T(8,128)(2,1)}, bf16[256,128]{0,1:T(8,128)(2,1)}) async-done(((bf16[256,128]{1,0:T(8,128)(2,1)}, bf16[256,128]{0,1:T(8,128)(2,1)}), (bf16[256,128]{1,0:T(8,128)(2,1)}, bf16[256,128]{0,1:T(8,128)(2,1)})) %all-reduce.3.cloned.1.call-update) | async-done | bytes 131088 | tf_op jit(solution)/shard_map/psum | solution.py:11
  166.8 2.1 fusion.208
  168.9 1.3 fusion.210
  170.2 1.3 fusion.213
  171.5 1.1 fusion.214
  172.7 1.3 subtract_exponential_fusion.3
  174.0 1.3 subtract_exponential_fusion.1
  175.3 2.0 fusion.96
  177.2 2.0 fusion.94
  179.2 1.0 fusion.86
  180.1 1.9 fusion.45
  182.0 2.9 fusion.34
  184.9 26.6 %all-gather.3.cloned.1.call-done = bf16[4096,1,128]{0,2,1:T(8,128)(2,1)} async-done(((bf16[256,1,128]{0,2,1:T(8,128)(2,1)}), bf16[4096,1,128]{0,2,1:T(8,128)(2,1)}) %all-gather.3.cloned.1.call-update) | async-done | bytes 1048592 | tf_op jit(solution)/shard_map/all_gather | solution.py:110
  211.5 8.2 %bitcast_reduce_fusion.3 = (f32[128,8]{0,1:T(8,128)S(1)}, f32[4096,128,8]{1,0,2:T(8,128)}) fusion(pred[4096]{0:T(1024)(128)(4,1)} %fusion.143, bf16[128,8,128]{0,2,1:T(8,128)(2,1)} %bitcast.345, bf16[4096,1,128]{0,2,1:T(8,128)(2,1)} %all-gather.3.cloned.1.call-done), kind=kOutput, calls=%fused_computation.13 | convolution fusion | flops 1086323712 | bytes 18096128 | tf_op jit(solution)/shard_map/tkrd,ckd->ktrc/dot_general | solution.py:17
  219.7 0.6 subtract_exponential_fusion.6
  220.3 0.7 fusion.118
  221.1 1.1 fusion.59
  222.1 34.8 %all-gather.5.cloned.1.call-done = bf16[4096,1,128]{0,2,1:T(8,128)(2,1)} async-done(((bf16[256,1,128]{0,2,1:T(8,128)(2,1)}), bf16[4096,1,128]{0,2,1:T(8,128)(2,1)}) %all-gather.5.cloned.1.call-update) | async-done | bytes 1048592 | tf_op jit(solution)/shard_map/all_gather | solution.py:111
  257.0 8.7 %fusion.22 = f32[128,8,128]{0,2,1:T(8,128)S(1)} fusion(f32[4096,128,8]{1,0,2:T(8,128)} %get-tuple-element.49, f32[128,8]{0,1:T(8,128)} %get-tuple-element.15, pred[4096]{0:T(1024)(128)(4,1)S(1)} %copy-done.40, bf16[4096,1,128]{0,2,1:T(8,128)(2,1)} %all-gather.5.cloned.1.call-done), kind=kOutput, calls=%fused_computation.31 | convolution fusion | flops 1094713344 | bytes 18358272 | tf_op jit(solution)/shard_map/ktrc,ckd->ktrd/dot_general | solution.py:26
  265.7 1.1 fusion.57
  266.8 2.1 copy.215
  268.9 3.7 %fusion.63 = f32[4096,128,8]{1,0,2:T(8,128)S(1)} fusion(bf16[128,8,128]{0,2,1:T(8,128)(2,1)S(1)} %bitcast.339, bf16[4096,1,128]{0,2,1:T(8,128)(2,1)} %all-gather.3.cloned.1.call-done), kind=kOutput, calls=%fused_computation.89 | convolution fusion | flops 1073741824 | bytes 18087936 | tf_op jit(solution)/shard_map/tkrd,ckd->ktrc/dot_general | solution.py:17
  272.6 8.6 %fusion.65 = f32[4096,128,8]{1,0,2:T(8,128)} fusion(bf16[128,8,128]{0,2,1:T(8,128)(2,1)S(1)} %bitcast.342, bf16[4096,1,128]{0,2,1:T(8,128)(2,1)S(1)} %copy-done.7), kind=kOutput, calls=%fused_computation.91 | convolution fusion | flops 1073741824 | bytes 18087936 | tf_op jit(solution)/shard_map/tkrd,ckd->ktrc/dot_general | solution.py:17
  281.2 24.2 %fusion.8 = (f32[128,8]{0,1:T(8,128)S(1)}, f32[128,8]{0,1:T(8,128)S(1)}, f32[128,8]{0,1:T(8,128)S(1)}, f32[128,8]{0,1:T(8,128)S(1)}, f32[4096,128,8]{1,0,2:T(8,128)}) fusion(f32[4096,128,8]{1,0,2:T(8,128)} %get-tuple-element.49, f32[128,8]{0,1:T(8,128)S(1)} %copy-done.54, pred[4096]{0:T(1024)(128)(4,1)S(1)} %copy-done.40, f32[4096,128,8]{1,0,2:T(8,128)} %fusion.65, ...), kind=kOutput, calls=%fused_computation.20 | convolution fusion | flops 1132457984 | bytes 68444160 | tf_op jit(solution)/shard_map/tkrd,ckd->ktrc/dot_general | solution.py:17
  305.5 1.6 fusion.80
  307.1 1.4 fusion.82
  308.5 1.5 fusion.58
  310.1 8.5 %fusion.20 = f32[128,8,128]{0,2,1:T(8,128)S(1)} fusion(f32[4096,128,8]{1,0,2:T(8,128)} %get-tuple-element.54, f32[128,8]{0,1:T(8,128)S(1)} %get-tuple-element.18, pred[4096]{0:T(1024)(128)(4,1)S(1)} %copy-done.40, bf16[4096,1,128]{0,2,1:T(8,128)(2,1)} %all-gather.5.cloned.1.call-done), kind=kOutput, calls=%fused_computation.30 | convolution fusion | flops 1094713344 | bytes 18358272 | tf_op jit(solution)/shard_map/ktrc,ckd->ktrd/dot_general | solution.py:26
  318.6 0.3 fusion.55
  319.0 0.2 copy.216
  319.2 8.5 %fusion.18 = f32[128,8,128]{0,2,1:T(8,128)S(1)} fusion(f32[4096,128,8]{1,0,2:T(8,128)} %fusion.65, f32[128,8]{0,1:T(8,128)S(1)} %get-tuple-element.72, pred[4096]{0:T(1024)(128)(4,1)S(1)} %copy-done.40, bf16[4096,1,128]{0,2,1:T(8,128)(2,1)} %all-gather.5.cloned.1.call-done), kind=kOutput, calls=%fused_computation.29 | convolution fusion | flops 1094713344 | bytes 18358272 | tf_op jit(solution)/shard_map/ktrc,ckd->ktrd/dot_general | solution.py:26
  327.8 0.6 fusion.53
  328.4 0.2 copy.217
  328.6 19.5 %fusion.10 = (f32[128,8]{0,1:T(8,128)S(1)}, f32[128,8]{0,1:T(8,128)S(1)}, f32[128,8]{0,1:T(8,128)S(1)}) fusion(f32[4096,128,8]{1,0,2:T(8,128)} %get-tuple-element.54, f32[128,8]{0,1:T(8,128)S(1)} %get-tuple-element.18, pred[4096]{0:T(1024)(128)(4,1)S(1)} %copy-done.41, f32[128,8]{0,1:T(8,128)S(1)} %get-tuple-element.72, f32[4096,128,8]{1,0,2:T(8,128)} %fusion.65, ...), kind=kLoop, calls=%fused_computation.22 | loop fusion | flops 62911488 | bytes 50360320 | tf_op jit(solution)/shard_map/reduce_sum | solution.py:24
  348.3 8.4 %fusion.16 = f32[128,8,128]{0,2,1:T(8,128)S(1)} fusion(f32[4096,128,8]{1,0,2:T(8,128)} %copy-done.2, f32[128,8]{0,1:T(8,128)S(1)} %get-tuple-element.27, pred[4096]{0:T(1024)(128)(4,1)S(1)} %copy-done.41, bf16[4096,1,128]{0,2,1:T(8,128)(2,1)S(1)} %copy-done.57), kind=kOutput, calls=%fused_computation.28 | convolution fusion | flops 1094713344 | bytes 18358272 | tf_op jit(solution)/shard_map/ktrc,ckd->ktrd/dot_general | solution.py:26
  356.9 0.8 fusion.61
  357.6 0.2 copy.218
  358.1 0.1 copy.219
  358.2 0.6 div.28
  358.8 1.6 fusion.32
  (139 shorter events, 0.8 us)
Async XLA Ops:
  6.5 0.9 copy-start
  8.1 10.2 %all-to-all-start.1 = ((bf16[64,8,128]{2,0,1:T(8,128)(2,1)}), bf16[64,8,128]{2,0,1:T(8,128)(2,1)S(1)}, u32[]{:S(2)}, u32[]{:S(2)}) async-start(bf16[64,8,128]{2,0,1:T(8,128)(2,1)} %copy_bitcast_fusion), calls=%async_computation.1 | async-start | bytes 262144 | tf_op jit(solution)/shard_map/all_to_all | solution.py:65
  18.3 15.6 %copy-start.15 = (bf16[64,8,128]{2,0,1:T(8,128)(2,1)}, bf16[64,8,128]{2,0,1:T(8,128)(2,1)S(1)}, u32[]{:S(2)}) copy-start(bf16[64,8,128]{2,0,1:T(8,128)(2,1)S(1)} %all-to-all-done.1) | copy-start | bytes 393220
  18.3 8.8 %all-to-all-start = ((bf16[64,8,128]{2,0,1:T(8,128)(2,1)}), bf16[64,8,128]{2,0,1:T(8,128)(2,1)S(1)}, u32[]{:S(2)}, u32[]{:S(2)}) async-start(bf16[64,8,128]{2,0,1:T(8,128)(2,1)} %copy_bitcast_fusion.1), calls=%async_computation | async-start | bytes 262144 | tf_op jit(solution)/shard_map/all_to_all | solution.py:64
  21.7 145.1 %all-reduce.3.cloned.1.call-start = ((), (), s32[]{:S(2)}) async-start(), calls=%async_computation.4 | async-start | bytes 262144 | tf_op jit(solution)/shard_map/psum | solution.py:11
  27.8 183.7 %all-gather.3.cloned.1.call-start = ((), (), s32[]{:S(2)}) async-start(), calls=%async_computation.2 | async-start | bytes 1114112 | tf_op jit(solution)/shard_map/all_gather | solution.py:110
  29.6 227.4 %all-gather.5.cloned.1.call-start = ((), (), s32[]{:S(2)}) async-start(), calls=%async_computation.3 | async-start | bytes 1114112 | tf_op jit(solution)/shard_map/all_gather | solution.py:111
  31.1 135.7 %copy-start.8 = (bf16[128,1024]{0,1:T(8,128)(2,1)}, bf16[128,1024]{0,1:T(8,128)(2,1)S(1)}, u32[]{:S(2)}) copy-start(bf16[128,1024]{0,1:T(8,128)(2,1)S(1)} %copy.259) | copy-start | bytes 786436
  31.4 135.4 %copy-start.5 = (bf16[128,1024]{0,1:T(8,128)(2,1)}, bf16[128,1024]{0,1:T(8,128)(2,1)S(1)}, u32[]{:S(2)}) copy-start(bf16[128,1024]{0,1:T(8,128)(2,1)S(1)} %copy.261) | copy-start | bytes 786436
  31.6 135.2 %copy-start.9 = (bf16[128,1024]{0,1:T(8,128)(2,1)}, bf16[128,1024]{0,1:T(8,128)(2,1)S(1)}, u32[]{:S(2)}) copy-start(bf16[128,1024]{0,1:T(8,128)(2,1)S(1)} %copy.260) | copy-start | bytes 786436
  32.4 134.4 %copy-start.21 = (pred[128,256]{0,1:T(8,128)(4,1)}, pred[128,256]{0,1:T(8,128)(4,1)S(1)}, u32[]{:S(2)}) copy-start(pred[128,256]{0,1:T(8,128)(4,1)S(1)} %iota_compare_fusion.3) | copy-start | bytes 98308
  32.5 134.3 %copy-start.17 = (pred[128,384]{1,0:T(8,128)(4,1)}, pred[128,384]{1,0:T(8,128)(4,1)S(1)}, u32[]{:S(2)}) copy-start(pred[128,384]{1,0:T(8,128)(4,1)S(1)} %iota_compare_fusion.2) | copy-start | bytes 147460
  32.6 134.2 %copy-start.19 = (pred[128,512]{1,0:T(8,128)(4,1)}, pred[128,512]{1,0:T(8,128)(4,1)S(1)}, u32[]{:S(2)}) copy-start(pred[128,512]{1,0:T(8,128)(4,1)S(1)} %iota_compare_fusion.1) | copy-start | bytes 196612
  40.2 179.5 %copy-start.28 = (f32[128,8]{0,1:T(8,128)S(1)}, f32[128,8]{0,1:T(8,128)}, u32[]{:S(2)}) copy-start(f32[128,8]{0,1:T(8,128)} %get-tuple-element.52) | copy-start | bytes 12292
  40.2 180.8 %copy-start.26 = (bf16[2,64,128]{2,1,0:T(8,128)(2,1)S(1)}, bf16[2,64,128]{2,1,0:T(8,128)(2,1)}, u32[]{:S(2)}) copy-start(bf16[2,64,128]{2,1,0:T(8,128)(2,1)} %slice.69) | copy-start | bytes 98308
  168.9 51.4 %copy-start.32 = (f32[128,8]{0,1:T(8,128)}, f32[128,8]{0,1:T(8,128)S(1)}, u32[]{:S(2)}) copy-start(f32[128,8]{0,1:T(8,128)S(1)} %get-tuple-element.50) | copy-start | bytes 12292
  168.9 88.0 %copy-start.40 = (pred[4096]{0:T(1024)(128)(4,1)S(1)}, pred[4096]{0:T(1024)(128)(4,1)}, u32[]{:S(2)}) copy-start(pred[4096]{0:T(1024)(128)(4,1)} %fusion.143) | copy-start | bytes 12292
  170.2 135.2 %copy-start.30 = (f32[128,8]{0,1:T(8,128)}, f32[128,8]{0,1:T(8,128)S(1)}, u32[]{:S(2)}) copy-start(f32[128,8]{0,1:T(8,128)S(1)} %get-tuple-element.55) | copy-start | bytes 12292
  171.5 2.5 copy-start.38
  172.7 47.0 %copy-start.36 = (f32[128,8]{0,1:T(8,128)}, f32[128,8]{0,1:T(8,128)S(1)}, u32[]{:S(2)}) copy-start(f32[128,8]{0,1:T(8,128)S(1)} %get-tuple-element.65) | copy-start | bytes 12292
  175.3 45.8 %copy-start.48 = (f32[128,8]{0,1:T(8,128)}, f32[128,8]{0,1:T(8,128)S(1)}, u32[]{:S(2)}) copy-start(f32[128,8]{0,1:T(8,128)S(1)} %get-tuple-element.47) | copy-start | bytes 12292
  219.7 1.3 copy-start.52
  221.0 44.6 %copy-start.14 = (bf16[256,128]{0,1:T(8,128)(2,1)S(1)}, bf16[256,128]{0,1:T(8,128)(2,1)}, u32[]{:S(2)}) copy-start(bf16[256,128]{0,1:T(8,128)(2,1)} %get-tuple-element.13) | copy-start | bytes 196612
  221.0 44.6 %copy-start.47 = (f32[128,8]{0,1:T(8,128)S(1)}, f32[128,8]{0,1:T(8,128)}, u32[]{:S(2)}) copy-start(f32[128,8]{0,1:T(8,128)} %get-tuple-element.14) | copy-start | bytes 12292
  257.0 8.7 %copy-start.3 = (f32[128,8,256]{0,2,1:T(8,128)S(1)}, f32[128,8,256]{0,2,1:T(8,128)}, u32[]{:S(2)}) copy-start(f32[128,8,256]{0,2,1:T(8,128)} %get-tuple-element.51) | copy-start | bytes 3145732
  257.0 8.7 %copy-start.13 = (f32[128,8,128]{0,2,1:T(8,128)S(1)}, f32[128,8,128]{0,2,1:T(8,128)}, u32[]{:S(2)}) copy-start(f32[128,8,128]{0,2,1:T(8,128)} %fusion.59) | copy-start | bytes 1572868
  265.6 6.9 %copy-start.6 = (bf16[128,1024]{0,1:T(8,128)(2,1)S(1)}, bf16[128,1024]{0,1:T(8,128)(2,1)}, u32[]{:S(2)}) copy-start(bf16[128,1024]{0,1:T(8,128)(2,1)} %copy-done.5) | copy-start | bytes 786436
  268.9 3.7 %copy-start.7 = (bf16[4096,1,128]{0,2,1:T(8,128)(2,1)S(1)}, bf16[4096,1,128]{0,2,1:T(8,128)(2,1)}, u32[]{:S(2)}) copy-start(bf16[4096,1,128]{0,2,1:T(8,128)(2,1)} %all-gather.3.cloned.1.call-done) | copy-start | bytes 3145732
  268.9 12.3 %copy-start.10 = (bf16[128,1024]{0,1:T(8,128)(2,1)S(1)}, bf16[128,1024]{0,1:T(8,128)(2,1)}, u32[]{:S(2)}) copy-start(bf16[128,1024]{0,1:T(8,128)(2,1)} %copy-done.9) | copy-start | bytes 786436
  268.9 12.3 %copy-start.54 = (f32[128,8]{0,1:T(8,128)S(1)}, f32[128,8]{0,1:T(8,128)}, u32[]{:S(2)}) copy-start(f32[128,8]{0,1:T(8,128)} %get-tuple-element.15) | copy-start | bytes 12292
  272.6 32.8 %copy-start.2 = (f32[4096,128,8]{1,0,2:T(8,128)}, f32[4096,128,8]{1,0,2:T(8,128)S(1)}, u32[]{:S(2)}) copy-start(f32[4096,128,8]{1,0,2:T(8,128)S(1)} %fusion.63) | copy-start | bytes 50331652
  281.2 24.2 %copy-start.27 = (f32[128,8]{0,1:T(8,128)S(1)}, f32[128,8]{0,1:T(8,128)}, u32[]{:S(2)}) copy-start(f32[128,8]{0,1:T(8,128)} %get-tuple-element.57) | copy-start | bytes 12292
  281.2 25.9 %copy-start.22 = (pred[128,256]{0,1:T(8,128)(4,1)S(1)}, pred[128,256]{0,1:T(8,128)(4,1)}, u32[]{:S(2)}) copy-start(pred[128,256]{0,1:T(8,128)(4,1)} %copy-done.21) | copy-start | bytes 98308
  281.2 27.3 %copy-start.25 = (bf16[4,64,128]{2,1,0:T(8,128)(2,1)S(1)}, bf16[4,64,128]{2,1,0:T(8,128)(2,1)}, u32[]{:S(2)}) copy-start(bf16[4,64,128]{2,1,0:T(8,128)(2,1)} %get-tuple-element.32) | copy-start | bytes 196612
  318.9 8.8 %copy-start.12 = (f32[128,8,128]{0,2,1:T(8,128)S(1)}, f32[128,8,128]{0,2,1:T(8,128)}, u32[]{:S(2)}) copy-start(f32[128,8,128]{0,2,1:T(8,128)} %fusion.96) | copy-start | bytes 1572868
  318.9 8.8 %copy-start.18 = (pred[128,384]{1,0:T(8,128)(4,1)S(1)}, pred[128,384]{1,0:T(8,128)(4,1)}, u32[]{:S(2)}) copy-start(pred[128,384]{1,0:T(8,128)(4,1)} %copy-done.17) | copy-start | bytes 147460
  319.0 8.8 %copy-start.24 = (bf16[6,64,128]{2,1,0:T(8,128)(2,1)S(1)}, bf16[6,64,128]{2,1,0:T(8,128)(2,1)}, u32[]{:S(2)}) copy-start(bf16[6,64,128]{2,1,0:T(8,128)(2,1)} %slice.75) | copy-start | bytes 294916
  319.0 8.8 %copy-start.50 = (f32[128,8]{0,1:T(8,128)S(1)}, f32[128,8]{0,1:T(8,128)}, u32[]{:S(2)}) copy-start(f32[128,8]{0,1:T(8,128)} %get-tuple-element.20) | copy-start | bytes 12292
  319.0 8.8 %copy-start.51 = (f32[128,8]{0,1:T(8,128)S(1)}, f32[128,8]{0,1:T(8,128)}, u32[]{:S(2)}) copy-start(f32[128,8]{0,1:T(8,128)} %get-tuple-element.44) | copy-start | bytes 12292
  319.2 9.4 %copy-start.41 = (pred[4096]{0:T(1024)(128)(4,1)S(1)}, pred[4096]{0:T(1024)(128)(4,1)}, u32[]{:S(2)}) copy-start(pred[4096]{0:T(1024)(128)(4,1)} %fusion.143) | copy-start | bytes 12292
  328.6 19.5 %copy-start.57 = (bf16[4096,1,128]{0,2,1:T(8,128)(2,1)S(1)}, bf16[4096,1,128]{0,2,1:T(8,128)(2,1)}, u32[]{:S(2)}) copy-start(bf16[4096,1,128]{0,2,1:T(8,128)(2,1)} %all-gather.5.cloned.1.call-done) | copy-start | bytes 3145732
  328.6 31.8 %copy-start.1 = (bf16[64,1024]{1,0:T(8,128)(2,1)S(1)}, bf16[64,1024]{1,0:T(8,128)(2,1)}, u32[]{:S(2)}) copy-start(bf16[64,1024]{1,0:T(8,128)(2,1)} %param.6) | copy-start | bytes 393220
  348.1 8.7 %copy-start.4 = (f32[128,8,512]{2,0,1:T(8,128)S(1)}, f32[128,8,512]{2,0,1:T(8,128)}, u32[]{:S(2)}) copy-start(f32[128,8,512]{2,0,1:T(8,128)} %get-tuple-element.64) | copy-start | bytes 6291460
  348.1 8.7 %copy-start.16 = (bf16[64,8,128]{2,0,1:T(8,128)(2,1)S(1)}, bf16[64,8,128]{2,0,1:T(8,128)(2,1)}, u32[]{:S(2)}) copy-start(bf16[64,8,128]{2,0,1:T(8,128)(2,1)} %copy-done.15) | copy-start | bytes 393220
  348.2 8.7 %copy-start.20 = (pred[128,512]{1,0:T(8,128)(4,1)S(1)}, pred[128,512]{1,0:T(8,128)(4,1)}, u32[]{:S(2)}) copy-start(pred[128,512]{1,0:T(8,128)(4,1)} %copy-done.19) | copy-start | bytes 196612
  348.2 8.7 %copy-start.23 = (f32[128,8,128]{0,2,1:T(8,128)S(1)}, f32[128,8,128]{0,2,1:T(8,128)}, u32[]{:S(2)}) copy-start(f32[128,8,128]{0,2,1:T(8,128)} %fusion.94) | copy-start | bytes 1572868
  348.2 8.7 %copy-start.49 = (f32[128,8]{0,1:T(8,128)S(1)}, f32[128,8]{0,1:T(8,128)}, u32[]{:S(2)}) copy-start(f32[128,8]{0,1:T(8,128)} %copy-done.48) | copy-start | bytes 12292
  348.2 8.7 %copy-start.55 = (f32[128,8]{0,1:T(8,128)S(1)}, f32[128,8]{0,1:T(8,128)}, u32[]{:S(2)}) copy-start(f32[128,8]{0,1:T(8,128)} %get-tuple-element.24) | copy-start | bytes 12292
  348.2 8.7 %copy-start.56 = (f32[128,8]{0,1:T(8,128)S(1)}, f32[128,8]{0,1:T(8,128)}, u32[]{:S(2)}) copy-start(f32[128,8]{0,1:T(8,128)} %get-tuple-element.45) | copy-start | bytes 12292
  348.2 9.6 %copy-start.29 = (f32[128,8]{0,1:T(8,128)S(1)}, f32[128,8]{0,1:T(8,128)}, u32[]{:S(2)}) copy-start(f32[128,8]{0,1:T(8,128)} %get-tuple-element.52) | copy-start | bytes 12292
  348.2 9.6 %copy-start.33 = (f32[128,8]{0,1:T(8,128)S(1)}, f32[128,8]{0,1:T(8,128)}, u32[]{:S(2)}) copy-start(f32[128,8]{0,1:T(8,128)} %copy-done.32) | copy-start | bytes 12292
  348.2 9.6 %copy-start.46 = (f32[128,8]{0,1:T(8,128)S(1)}, f32[128,8]{0,1:T(8,128)}, u32[]{:S(2)}) copy-start(f32[128,8]{0,1:T(8,128)} %fusion.118) | copy-start | bytes 12292
  348.2 9.6 %copy-start.53 = (f32[128,8]{0,1:T(8,128)S(1)}, f32[128,8]{0,1:T(8,128)}, u32[]{:S(2)}) copy-start(f32[128,8]{0,1:T(8,128)} %copy-done.52) | copy-start | bytes 12292
  348.2 9.7 %copy-start.31 = (f32[128,8]{0,1:T(8,128)S(1)}, f32[128,8]{0,1:T(8,128)}, u32[]{:S(2)}) copy-start(f32[128,8]{0,1:T(8,128)} %copy-done.30) | copy-start | bytes 12292
  348.3 9.7 %copy-start.35 = (f32[128,8]{0,1:T(8,128)S(1)}, f32[128,8]{0,1:T(8,128)}, u32[]{:S(2)}) copy-start(f32[128,8]{0,1:T(8,128)} %get-tuple-element.59) | copy-start | bytes 12292
  348.3 9.7 %copy-start.39 = (f32[128,8]{0,1:T(8,128)S(1)}, f32[128,8]{0,1:T(8,128)}, u32[]{:S(2)}) copy-start(f32[128,8]{0,1:T(8,128)} %copy-done.38) | copy-start | bytes 12292
  348.3 9.7 %copy-start.44 = (f32[128,8]{0,1:T(8,128)S(1)}, f32[128,8]{0,1:T(8,128)}, u32[]{:S(2)}) copy-start(f32[128,8]{0,1:T(8,128)} %get-tuple-element.69) | copy-start | bytes 12292
  348.3 9.7 %copy-start.45 = (f32[128,8]{0,1:T(8,128)S(1)}, f32[128,8]{0,1:T(8,128)}, u32[]{:S(2)}) copy-start(f32[128,8]{0,1:T(8,128)} %fusion.45) | copy-start | bytes 12292
  348.3 9.7 %copy-start.34 = (f32[128,8]{0,1:T(8,128)S(1)}, f32[128,8]{0,1:T(8,128)}, u32[]{:S(2)}) copy-start(f32[128,8]{0,1:T(8,128)} %get-tuple-element.63) | copy-start | bytes 12292
  348.3 9.7 %copy-start.37 = (f32[128,8]{0,1:T(8,128)S(1)}, f32[128,8]{0,1:T(8,128)}, u32[]{:S(2)}) copy-start(f32[128,8]{0,1:T(8,128)} %copy-done.36) | copy-start | bytes 12292
  348.3 9.7 %copy-start.42 = (f32[128,8]{0,1:T(8,128)S(1)}, f32[128,8]{0,1:T(8,128)}, u32[]{:S(2)}) copy-start(f32[128,8]{0,1:T(8,128)} %get-tuple-element.70) | copy-start | bytes 12292
  348.3 9.7 %copy-start.43 = (f32[128,8]{0,1:T(8,128)S(1)}, f32[128,8]{0,1:T(8,128)}, u32[]{:S(2)}) copy-start(f32[128,8]{0,1:T(8,128)} %fusion.34) | copy-start | bytes 12292
  348.3 10.5 %copy-start.11 = (f32[128,1024]{1,0:T(8,128)S(1)}, f32[128,1024]{1,0:T(8,128)}, u32[]{:S(2)}) copy-start(f32[128,1024]{1,0:T(8,128)} %copy.215) | copy-start | bytes 1572868
Sparse Core Ops, SparseCore 0:
  27.9 138.8 all-reduce.2
  169.4 42.0 all-gather.2
  214.1 42.8 all-gather.4
where the time goes:
time: 372 us; the launch traced here: 367 us
  waiting for transfers between devices  196 us (53%)
  matrix products  101 us (27%)
  other arithmetic  36 us (10%)
  between operations  14.1 us (4%)
  local copies, waits for them, and re-layouts  11.4 us (3%)
  starting transfers between devices  8.23 us (2%)
    psum x1, waiting for transfers between devices, spread(): return lax.psum(block, axis)  127 us
    dot_general x12, matrix products, refresh(): jnp.einsum('tkrd,ckd->ktrc', block_queries, block_keys, preferred_element...  56.8 us
    dot_general x12, matrix products, refresh(): jnp.einsum('ktrc,ckd->ktrd', weights, block_values, preferred_element_typ...  43.5 us
    all_gather x1, waiting for transfers between devices, local(): lax.all_gather(pass_values, 'seq', axis=0, tiled=True)  34.8 us
    reduce_sum x7, other arithmetic, refresh(): totals = totals * rescale + jnp.sum(exps, axis=-1)  28.9 us
    all_gather x1, waiting for transfers between devices, local(): lax.all_gather(pass_keys, 'seq', axis=0, tiled=True)  26.6 us
  transfers between devices with their start and end apart: 5, of which 5 were waited for; matrix products, arithmetic and copies ran while one was open for 12% of the time, Pallas kernels for 0%

commit v1 on v0

v1 whole, which is shorter than its diff:
```python
import functools

import jax
import jax.numpy as jnp
from jax import lax
from jax.experimental import pallas as pl
from jax.experimental.pallas import tpu as pltpu
from jax.sharding import PartitionSpec as P

HD = 128
GROUP = 8
BLK = 512
PASS = 256
ANCHOR = 256
SCALE = float(HD**-0.5 * 1.4426950408889634)
LIMIT = 1e30
BF16, F32 = jnp.bfloat16, jnp.float32
NT = (((1,), (1,)), ((), ()))
VMEM_BYTES = 40 * 2**20
UNROLL = 2


def full(count):
    return [pl.BlockSpec(memory_space=pltpu.VMEM)] * count


def cost(units):
    return pl.CostEstimate(
        flops=int(units * 2 * 2 * GROUP * BLK * 256 * 256),
        bytes_accessed=1 << 20,
        transcendentals=int(units * GROUP * BLK * 256),
    )


def params():
    return pltpu.CompilerParams(vmem_limit_bytes=VMEM_BYTES)


def select_kernel(rows_ref, kv_ref, out_ref):
    rows = rows_ref[...]
    ids = lax.broadcasted_iota(jnp.int32, (BLK, PASS), 0)
    picked = jnp.where(ids == rows, 1.0, 0.0).astype(BF16)
    out_ref[...] = lax.dot_general(
        picked, kv_ref[...], (((0,), (0,)), ((), ())), preferred_element_type=F32
    ).astype(BF16)


def select(rows, kv):
    return pl.pallas_call(
        select_kernel,
        out_shape=jax.ShapeDtypeStruct((PASS, 2 * HD), BF16),
        in_specs=full(2),
        out_specs=pl.BlockSpec(memory_space=pltpu.VMEM),
        compiler_params=params(),
        name="select_rows",
    )(rows, kv)


def widen(wide, at, kv):
    count = kv.shape[0]
    wide[at : at + count, :HD] = kv[:, HD:]
    wide[at : at + count, HD:] = jnp.ones((count, HD), BF16)


def powers(scores, shift):
    parts = [
        jnp.exp2(scores[:, j : j + HD] * SCALE - shift) for j in range(0, scores.shape[1], HD)
    ]
    return jnp.concatenate([part.astype(BF16) for part in parts], axis=1)


def heads(body):
    def step(r, carry):
        body(r)
        return carry

    lax.fori_loop(0, GROUP, step, 0, unroll=UNROLL)


def columns(r):
    return pl.ds(pl.multiple_of(r * HD, HD), HD)


def local_kernel(q_ref, kv_ref, acc_ref, shift_ref, wide):
    widen(wide, 0, kv_ref[...])
    half = BLK // 2
    ones = jnp.ones((HD, HD), BF16)
    rows = lax.broadcasted_iota(jnp.int32, (half, half), 0)
    cols = lax.broadcasted_iota(jnp.int32, (half, half), 1)
    causal = cols <= rows

    def body(r):
        q = q_ref[:, columns(r)]
        k = kv_ref[:, :HD]
        own = (q.astype(F32) * k.astype(F32)).astype(BF16)
        shift = jnp.dot(own, ones, preferred_element_type=F32) * SCALE
        shift_ref[r] = shift
        for t in range(2):
            tile = slice(t * half, (t + 1) * half)
            weights = []
            for u in range(t + 1):
                scores = lax.dot_general(
                    q[tile], k[u * half : (u + 1) * half], NT, preferred_element_type=F32
                )
                if u == t:
                    scores = jnp.where(causal, scores, -jnp.inf)
                weights.append(powers(scores, shift[tile]))
            weights = jnp.concatenate(weights, axis=1)
            acc_ref[r, tile] = jnp.dot(
                weights, wide[: (t + 1) * half], preferred_element_type=F32
            )

    heads(body)


def local_part(q, kv):
    return pl.pallas_call(
        local_kernel,
        out_shape=(
            jax.ShapeDtypeStruct((GROUP, BLK, 2 * HD), F32),
            jax.ShapeDtypeStruct((GROUP, BLK, HD), F32),
        ),
        in_specs=full(2),
        out_specs=tuple(full(2)),
        scratch_shapes=[pltpu.VMEM((BLK, 2 * HD), BF16)],
        compiler_params=params(),
        cost_estimate=cost(1.5),
        name="local_block",
    )(q, kv)


def add_keys(q_ref, acc_ref, shift_ref, refs, keys, wide):
    at = 0
    for ref in refs:
        kv = ref[...]
        keys[at : at + kv.shape[0]] = kv[:, :HD]
        widen(wide, at, kv)
        at += kv.shape[0]

    def body(r):
        scores = lax.dot_general(
            q_ref[:, columns(r)], keys[:at], NT, preferred_element_type=F32
        )
        weights = powers(scores, shift_ref[r])
        acc_ref[r] += jnp.dot(weights, wide[:at], preferred_element_type=F32)

    heads(body)


def stage_kernel(groups, use_ref, q_ref, shift_ref, *refs):
    count = sum(groups)
    kv_refs, (_, acc_ref, keys, wide) = refs[:count], refs[count:]
    at = 0
    for g, size in enumerate(groups):
        members = kv_refs[at : at + size]
        at += size

        @pl.when(use_ref[g] != 0)
        def _():
            add_keys(q_ref, acc_ref, shift_ref, members, keys, wide)


def stage(use, q, shift, acc, groups):
    flat = [x for group in groups for x in group]
    rows = max(sum(x.shape[0] for x in group) for group in groups)
    units = sum(x.shape[0] for x in flat) / 256
    return pl.pallas_call(
        functools.partial(stage_kernel, [len(group) for group in groups]),
        out_shape=jax.ShapeDtypeStruct(acc.shape, F32),
        in_specs=[pl.BlockSpec(memory_space=pltpu.SMEM)] + full(3 + len(flat)),
        out_specs=pl.BlockSpec(memory_space=pltpu.VMEM),
        scratch_shapes=[pltpu.VMEM((rows, HD), BF16), pltpu.VMEM((rows, 2 * HD), BF16)],
        input_output_aliases={3 + len(flat): 0},
        compiler_params=params(),
        cost_estimate=cost(units),
        name="add_blocks",
    )(use, q, shift, *flat, acc)


def online(q, keys, values, usable, running):
    top, total, mixed = running
    scores = lax.dot_general(q, keys, NT, preferred_element_type=F32) * SCALE
    if usable is not None:
        scores = jnp.where(usable, scores, -jnp.inf)
    fresh = jnp.maximum(top, jnp.max(scores, axis=1, keepdims=True))
    rescale = jnp.exp2(top - fresh)
    weights = jnp.exp2(scores - fresh)
    total = total * rescale + jnp.sum(weights, axis=1, keepdims=True)
    mixed = mixed * rescale + jnp.dot(weights.astype(BF16), values, preferred_element_type=F32)
    return fresh, total, mixed


def final_kernel(groups, stages, use_ref, q_ref, shift_ref, *refs):
    count = sum(groups)
    kv_refs, (local_ref, acc_in, out_ref, acc_ref, keys, wide, worst) = refs[:count], refs[count:]
    acc_ref[...] = acc_in[...]
    at = 0
    for g, size in enumerate(groups):
        members = kv_refs[at : at + size]
        at += size
        if g not in stages:
            continue

        @pl.when(use_ref[g] != 0)
        def _():
            add_keys(q_ref, acc_ref, shift_ref, members, keys, wide)

    worst[...] = jnp.zeros_like(worst)

    def finish(r):
        total = acc_ref[r, :, HD:]
        worst[...] = jnp.maximum(worst[...], jnp.where(total < LIMIT, 0.0, 1.0))
        out_ref[:, columns(r)] = (acc_ref[r, :, :HD] / total).astype(BF16)

    heads(finish)

    @pl.when(jnp.max(worst[...]) > 0.0)
    def _():
        tile = 128

        def redo(step, carry):
            r, t = step // (BLK // tile), step % (BLK // tile)
            here = pl.ds(pl.multiple_of(t * tile, tile), tile)
            q = q_ref[here, columns(r)]
            running = (
                jnp.full((tile, 1), -1e30, F32),
                jnp.zeros((tile, 1), F32),
                jnp.zeros((tile, HD), F32),
            )
            rows = t * tile + lax.broadcasted_iota(jnp.int32, (tile, BLK), 0)
            cols = lax.broadcasted_iota(jnp.int32, (tile, BLK), 1)
            running = online(q, local_ref[:, :HD], local_ref[:, HD:], cols <= rows, running)
            at = 0
            for g, size in enumerate(groups):
                for ref in kv_refs[at : at + size]:
                    running = lax.cond(
                        use_ref[g] != 0,
                        lambda s, ref=ref: online(q, ref[:, :HD], ref[:, HD:], None, s),
                        lambda s: s,
                        running,
                    )
                at += size
            out_ref[here, columns(r)] = (running[2] / running[1]).astype(BF16)
            return carry

        lax.fori_loop(0, GROUP * (BLK // tile), redo, 0)


def final(use, q, shift, acc, local_kv, groups, stages):
    flat = [x for group in groups for x in group]
    sizes = [sum(x.shape[0] for x in group) for group in groups]
    rows = max(sizes[g] for g in stages)
    units = sum(sizes[g] for g in stages) / 256
    return pl.pallas_call(
        functools.partial(final_kernel, [len(group) for group in groups], tuple(stages)),
        out_shape=jax.ShapeDtypeStruct((BLK, GROUP * HD), BF16),
        in_specs=[pl.BlockSpec(memory_space=pltpu.SMEM)] + full(4 + len(flat)),
        out_specs=pl.BlockSpec(memory_space=pltpu.VMEM),
        scratch_shapes=[
            pltpu.VMEM(acc.shape, F32),
            pltpu.VMEM((rows, HD), BF16),
            pltpu.VMEM((rows, 2 * HD), BF16),
            pltpu.VMEM((BLK, HD), F32),
        ],
        compiler_params=params(),
        cost_estimate=cost(units),
        name="last_blocks",
    )(use, q, shift, *flat, local_kv, acc)


def place(z, h, c):
    return 4 * z + 2 * h + c


SIBLING = [(s, s ^ 1) for s in range(16)]
PEER = [(s, s ^ 2) for s in range(16)]


def ahead(d):
    return [(s, s + 4 * d) for s in range(16 - 4 * d)]


def local(queries, key_states, value_states, passing_rows):
    me = lax.axis_index("seq")
    z, h, c = me // 4, (me // 2) % 2, me % 2
    move = functools.partial(lax.ppermute, axis_name="seq")

    heads_all = key_states.shape[1] // HD
    rows = key_states.shape[0]
    both = jnp.concatenate(
        [key_states.reshape(rows, heads_all, HD), value_states.reshape(rows, heads_all, HD)], axis=2
    ).transpose(1, 0, 2)
    kv = lax.all_to_all(both, "head", split_axis=0, concat_axis=0, tiled=True).reshape(BLK, 2 * HD)

    mine = select(passing_rows, kv)
    peer = move(mine, perm=PEER)
    acc, shift = local_part(queries, kv)

    anchor = kv[:ANCHOR]
    anchor_peer = move(anchor, perm=[(place(0, 0, 0), place(0, 1, 0))])
    anchor = jnp.where(me == place(0, 1, 0), anchor_peer, anchor)
    anchor_side = move(anchor, perm=[(place(0, 0, 0), place(0, 0, 1)), (place(0, 1, 0), place(0, 1, 1))])
    anchor = jnp.where((z == 0) & (c == 1), anchor_side, anchor)
    onward = move(
        anchor,
        perm=[(place(0, y, 0), place(1, y, 0)) for y in range(2)]
        + [(place(0, y, 1), place(2, y, 1)) for y in range(2)],
    )
    onward_side = move(
        onward,
        perm=[(place(1, y, 0), place(1, y, 1)) for y in range(2)]
        + [(place(2, y, 1), place(2, y, 0)) for y in range(2)],
    )
    half = jnp.where(c == 0, anchor[: ANCHOR // 2], anchor[ANCHOR // 2 :])

    pair = jnp.concatenate([mine, peer], axis=0)
    one = move(pair, perm=ahead(1))
    three = move(jnp.concatenate([pair, half], axis=0), perm=ahead(3))
    two = move(pair, perm=ahead(2))
    pair_side = move(pair, perm=SIBLING)
    one_side = move(one, perm=SIBLING)
    three_side = move(three, perm=SIBLING)
    two_side = move(two, perm=SIBLING)

    relayed = jnp.where(z == 0, anchor, jnp.where(((z == 1) & (c == 0)) | ((z == 2) & (c == 1)), onward, onward_side))

    def flags(*conditions):
        return jnp.stack([jnp.asarray(x).astype(jnp.int32) for x in conditions])

    near = [[peer, pair_side[PASS:]], [pair_side[:PASS]]]
    near_use = [h == 1, c == 1]
    acc = stage(flags(*near_use), queries, shift, acc, near)
    first = [[one, one_side]]
    acc = stage(flags(z >= 1), queries, shift, acc, first)
    rest = [[three, three_side], [relayed], [two, two_side]]
    rest_use = [z == 3, (me >= 1) & (z < 3), z >= 2]
    return final(
        flags(*(near_use + [z >= 1] + rest_use)),
        queries, shift, acc, kv, near + first + rest, [3, 4, 5],
    )


def solution(mesh):
    in_specs = (
        P("seq", "head"),
        P(("seq", "head"), None),
        P(("seq", "head"), None),
        P("head", "seq"),
    )
    return jax.shard_map(
        local, mesh=mesh, in_specs=in_specs, out_specs=P("seq", "head"), check_vma=False
    )
```

time: 372 us -> 182 us (0.49); the launches traced: 367 us -> 182 us
  waiting for transfers between devices: 196 us -> 7.17 us
  Pallas kernels: 0 us -> 148 us
  matrix products: 101 us -> 0 us
  other arithmetic: 36 us -> 0.24 us
  between operations: 14.1 us -> 0.31 us
  blocking collectives: 0 us -> 10.8 us
  local copies, waits for them, and re-layouts: 11.4 us -> 3.88 us
    pallas_call x0 -> x5, Pallas kernels: none -> 148 us  [the longest x1 133 us: final(): pl.pallas_call(functools.partial(final_kernel, [len(group) for group in g...]
    psum x1 -> x0, waiting for transfers between devices: 127 us -> none  [spread(): return lax.psum(block, axis)]
    dot_general x25 -> x0, matrix products: 101 us -> none  [the longest x12 56.8 us: refresh(): jnp.einsum('tkrd,ckd->ktrc', block_queries, block_keys, preferred_element...]
    all_gather x2 -> x0, waiting for transfers between devices: 61.4 us -> none  [the longest x1 34.8 us: local(): lax.all_gather(pass_values, 'seq', axis=0, tiled=True)]
    reduce_sum x7 -> x0, other arithmetic: 28.9 us -> none  [refresh(): totals = totals * rescale + jnp.sum(exps, axis=-1)]
    ppermute x0 -> x12, starting transfers between devices: none -> 11.3 us  [the longest x1 2.56 us: local(): pair_side = move(pair, perm=SIBLING)]
    all_to_all x0 -> x1, blocking collectives: none -> 10.8 us  [local(): lax.all_to_all(both, 'head', split_axis=0, concat_axis=0, tiled=True)]
    all_to_all x2 -> x0, starting transfers between devices: 8.11 us -> none  [the longest x1 4.74 us: local(): lax.all_to_all(value_states, 'head', split_axis=1, concat_axis=0, tiled=T...]
  transfers between devices with their start and end apart: 5 -> 12, of which waited for: 5 -> 2; matrix products, arithmetic and copies ran while one was open for 12% -> 0% of each run, Pallas kernels for 0% -> 9%
where the time goes in v1:
time: 182 us
  Pallas kernels  148 us (81%)
  starting transfers between devices  11.3 us (6%)
  blocking collectives  10.8 us (6%)
  waiting for transfers between devices  7.17 us (4%)
  local copies, waits for them, and re-layouts  3.88 us (2%)
    pallas_call x1, Pallas kernels, final(): pl.pallas_call(functools.partial(final_kernel, [len(group) for group in g...  133 us
    pallas_call x2, Pallas kernels, stage(): pl.pallas_call(functools.partial(stage_kernel, [len(group) for group in g...  11.8 us
    all_to_all x1, blocking collectives, local(): lax.all_to_all(both, 'head', split_axis=0, concat_axis=0, tiled=True)  10.8 us
    ppermute x1, waiting for transfers between devices, local(): one = move(pair, perm=ahead(1))  5.14 us
  transfers between devices with their start and end apart: 12, of which 2 were waited for; matrix products, arithmetic and copies ran while one was open for 0% of the time, Pallas kernels for 9%

profile of v1, /device:TPU:113, one launch (start us, length us, event | category | flops | bytes accessed | tf_op | source)
XLA Modules:
  0.0 182.1 jit_solution(12541096944230089735)
XLA Ops:
  0.0 0.0 copy-start
  0.0 0.9 copy-done
  0.9 1.0 copy_bitcast_fusion
  1.9 10.8 %all_to_all.5 = bf16[8,64,256]{2,1,0:T(8,128)(2,1)S(1)} all-to-all(bf16[8,64,256]{2,1,0:T(8,128)(2,1)S(1)} %maximum_bitcast_fusion), channel_id=1, replica_groups=mesh['seq'=16,'head'=8] {'head'}, dimensions={0} | all-to-all | bytes 524288 | tf_op jit(solution)/shard_map/all_to_all | solution.py:293
  12.8 0.7 collective-permute-start.4
  13.5 0.1 stack.56.use_ref
  13.6 0.1 pad_add_fusion.use_ref
  13.7 0.0 copy-start.2
  13.7 0.7 copy-done.2
  14.4 0.3 select_rows.1
  14.6 0.4 collective-permute-start
  15.1 0.0 collective-permute-done.4
  15.1 0.7 collective-permute-start.5
  15.8 0.0 copy-start.1
  15.8 1.2 copy-done.1
  17.0 3.6 %local_block.1 = (f32[8,512,256]{2,1,0:T(8,128)S(1)}, f32[8,512,128]{2,1,0:T(8,128)S(1)}) custom-call(bf16[512,1024]{1,0:T(8,128)(2,1)S(1)} %copy-done.1, bf16[512,256]{1,0:T(8,128)(2,1)S(1)} %bitcast.22), custom_call_target="tpu_custom_call" | custom-call | flops 1610612736 | bytes 1048576 | tf_op jit(solution)/shard_map/local_block/pallas_call | solution.py:117
  20.6 0.0 collective-permute-done.refs_0_
  20.7 2.6 %collective-permute-start.1 = (bf16[512,256]{1,0:T(8,128)(2,1)S(1)}, bf16[512,256]{1,0:T(8,128)(2,1)S(1)}, u32[]{:S(2)}, u32[]{:S(2)}) collective-permute-start(bf16[512,256]{1,0:T(8,128)(2,1)S(1)} %pad_maximum_fusion.1), channel_id=1, source_target_pairs={{0,8},{8,0},{16,24},{24,16},{32,40},{40,32},{48,56},{56,48},{64,72... | collective-permute-start | bytes 786440 | tf_op jit(solution)/shard_map/ppermute | solution.py:320
  23.2 1.3 collective-permute-start.2
  24.5 1.3 collective-permute-start.10
  25.8 0.0 collective-permute-done.5
  25.9 0.7 collective-permute-start.8
  26.6 1.3 collective-permute-start.6
  27.9 5.1 %collective-permute-done.2.refs_0_.refs_3_ = bf16[512,256]{1,0:T(8,128)(2,1)S(1)} collective-permute-done((bf16[512,256]{1,0:T(8,128)(2,1)S(1)}, bf16[512,256]{1,0:T(8,128)(2,1)S(1)}, u32[]{:S(2)}, u32[]{:S(2)}) %collective-permute-start.2) | collective-permute-done | bytes 262176 | tf_op jit(solution)/shard_map/ppermute | solution.py:317
  33.0 0.8 collective-permute-start.3
  33.8 2.0 %collective-permute-done.10.refs_8_ = bf16[512,256]{1,0:T(8,128)(2,1)S(1)} collective-permute-done((bf16[512,256]{1,0:T(8,128)(2,1)S(1)}, bf16[512,256]{1,0:T(8,128)(2,1)S(1)}, u32[]{:S(2)}, u32[]{:S(2)}) %collective-permute-start.10) | collective-permute-done | bytes 262176 | tf_op jit(solution)/shard_map/ppermute | solution.py:319
  35.8 0.9 collective-permute-start.11
  36.7 0.0 collective-permute-done.1
  36.8 0.0 collective-permute-done.8
  36.8 0.7 collective-permute-start.9
  37.5 6.2 %add_blocks.2.refs_2_ = f32[8,512,256]{2,1,0:T(8,128)S(1)} custom-call(s32[2]{0:T(128)S(1)} %pad_add_fusion.use_ref, bf16[512,1024]{1,0:T(8,128)(2,1)S(1)} %copy-done.1, f32[8,512,128]{2,1,0:T(8,128)S(1)} %get-tuple-element.7.shift_ref, bf16[256,256]{1,0:T(8,128)(2,1)S(1)} %collective-permute-done.refs_0_, ...), custom_call_target="tpu_custom_call", output_to_operand_aliasing={{}: (6, {})} | custom-call | flops 3221225472 | bytes 1048576 | tf_op jit(solution)/shard_map/add_blocks/pallas_call | solution.py:167
  43.6 0.0 collective-permute-done.9
  43.7 0.0 collective-permute-done.6.refs_5_
  43.7 0.1 collective-permute-start.7
  43.8 0.0 collective-permute-done.3.refs_1_.refs_4_
  43.8 5.6 %add_blocks.3.refs_11_ = f32[8,512,256]{2,1,0:T(8,128)S(1)} custom-call(s32[1]{0:T(128)} %bitcast.2.use_ref, bf16[512,1024]{1,0:T(8,128)(2,1)S(1)} %copy-done.1, f32[8,512,128]{2,1,0:T(8,128)S(1)} %get-tuple-element.7.shift_ref, bf16[512,256]{1,0:T(8,128)(2,1)S(1)} %collective-permute-done.2.refs_0_.refs_3_, ...), custom_call_target="tpu_custom_call", output_to_operand_aliasing={{}: (5, {})} | custom-call | flops 4294967296 | bytes 1048576 | tf_op jit(solution)/shard_map/add_blocks/pallas_call | solution.py:167
  49.4 0.0 collective-permute-done.11.refs_9_
  49.4 0.0 collective-permute-done.7.refs_6_
  49.4 132.7 %last_blocks.1 = bf16[512,1024]{1,0:T(8,128)(2,1)} custom-call(s32[6]{0:T(128)S(1)} %stack.56.use_ref, bf16[512,1024]{1,0:T(8,128)(2,1)S(1)} %copy-done.1, f32[8,512,128]{2,1,0:T(8,128)S(1)} %get-tuple-element.7.shift_ref, bf16[256,256]{1,0:T(8,128)(2,1)S(1)} %collective-permute-done.refs_0_, bf16[256,256]{1,0:T(8,128)(2,1)S(1)} %get-tuple-element.10.refs_1_, ...), custom_call_target="tpu_custom_call" | custom-call | flops 10737418240 | bytes 1048576 | tf_op jit(solution)/shard_map/last_blocks/pallas_call | solution.py:254
  (9 shorter events, 0.2 us)
Async XLA Ops:
  0.0 0.9 copy-start
  12.8 2.3 %collective-permute-start.4 = (bf16[256,256]{1,0:T(8,128)(2,1)S(1)}, bf16[256,256]{1,0:T(8,128)(2,1)S(1)}, u32[]{:S(2)}, u32[]{:S(2)}) collective-permute-start(bf16[256,256]{1,0:T(8,128)(2,1)S(1)} %bitcast.24), channel_id=1, source_target_pairs={{0,16},{1,17},{2,18},{3,19},{4,20},{5,21},{6,22},{7,23}} | collective-permute-start | bytes 393224 | tf_op jit(solution)/shard_map/ppermute | solution.py:300
  13.7 0.7 copy-start.2
  14.6 6.0 %collective-permute-start = (bf16[256,256]{1,0:T(8,128)(2,1)S(1)}, bf16[256,256]{1,0:T(8,128)(2,1)S(1)}, u32[]{:S(2)}, u32[]{:S(2)}) collective-permute-start(bf16[256,256]{1,0:T(8,128)(2,1)S(1)} %select_rows.1), channel_id=1, source_target_pairs={{0,16},{8,24},{16,0},{24,8},{32,48},{40,56},{48,32},{56,40},{64,80... | collective-permute-start | bytes 393224 | tf_op jit(solution)/shard_map/ppermute | solution.py:296
  15.1 10.7 %collective-permute-start.5 = (bf16[256,256]{1,0:T(8,128)(2,1)S(1)}, bf16[256,256]{1,0:T(8,128)(2,1)S(1)}, u32[]{:S(2)}, u32[]{:S(2)}) collective-permute-start(bf16[256,256]{1,0:T(8,128)(2,1)S(1)} %broadcast_select_fusion), channel_id=1, source_target_pairs={{0,8},{16,24},{1,9},{17,25},{2,10},{18,26},{3,11},{19,27},{4,12},{... | collective-permute-start | bytes 393224 | tf_op jit(solution)/shard_map/ppermute | solution.py:302
  15.8 1.2 copy-start.1
  20.7 16.1 %collective-permute-start.1 = (bf16[512,256]{1,0:T(8,128)(2,1)S(1)}, bf16[512,256]{1,0:T(8,128)(2,1)S(1)}, u32[]{:S(2)}, u32[]{:S(2)}) collective-permute-start(bf16[512,256]{1,0:T(8,128)(2,1)S(1)} %pad_maximum_fusion.1), channel_id=1, source_target_pairs={{0,8},{8,0},{16,24},{24,16},{32,40},{40,32},{48,56},{56,48},{64,72... | collective-permute-start | bytes 786440 | tf_op jit(solution)/shard_map/ppermute | solution.py:320
  23.2 9.8 %collective-permute-start.2 = (bf16[512,256]{1,0:T(8,128)(2,1)S(1)}, bf16[512,256]{1,0:T(8,128)(2,1)S(1)}, u32[]{:S(2)}, u32[]{:S(2)}) collective-permute-start(bf16[512,256]{1,0:T(8,128)(2,1)S(1)} %pad_maximum_fusion.1), channel_id=1, source_target_pairs={{0,32},{8,40},{16,48},{24,56},{32,64},{40,72},{48,80},{56,88},{64,... | collective-permute-start | bytes 786440 | tf_op jit(solution)/shard_map/ppermute | solution.py:317
  24.5 11.3 %collective-permute-start.10 = (bf16[512,256]{1,0:T(8,128)(2,1)S(1)}, bf16[512,256]{1,0:T(8,128)(2,1)S(1)}, u32[]{:S(2)}, u32[]{:S(2)}) collective-permute-start(bf16[512,256]{1,0:T(8,128)(2,1)S(1)} %pad_maximum_fusion.1), channel_id=1, source_target_pairs={{0,64},{8,72},{16,80},{24,88},{32,96},{40,104},{48,112},{56,120},{... | collective-permute-start | bytes 786440 | tf_op jit(solution)/shard_map/ppermute | solution.py:319
  25.9 10.9 %collective-permute-start.8 = (bf16[256,256]{1,0:T(8,128)(2,1)S(1)}, bf16[256,256]{1,0:T(8,128)(2,1)S(1)}, u32[]{:S(2)}, u32[]{:S(2)}) collective-permute-start(bf16[256,256]{1,0:T(8,128)(2,1)S(1)} %broadcast_select_fusion.1), channel_id=1, source_target_pairs={{0,32},{16,48},{8,72},{24,88},{1,33},{17,49},{9,73},{25,89},{2,34}... | collective-permute-start | bytes 393224 | tf_op jit(solution)/shard_map/ppermute | solution.py:304
  26.6 17.1 %collective-permute-start.6 = (bf16[640,256]{1,0:T(8,128)(2,1)S(1)}, bf16[640,256]{1,0:T(8,128)(2,1)S(1)}, u32[]{:S(2)}, u32[]{:S(2)}) collective-permute-start(bf16[640,256]{1,0:T(8,128)(2,1)S(1)} %pad_maximum_fusion), channel_id=1, source_target_pairs={{0,96},{8,104},{16,112},{24,120},{1,97},{9,105},{17,113},{25,121},... | collective-permute-start | bytes 983048 | tf_op jit(solution)/shard_map/ppermute | solution.py:318
  33.0 10.7 %collective-permute-start.3 = (bf16[512,256]{1,0:T(8,128)(2,1)S(1)}, bf16[512,256]{1,0:T(8,128)(2,1)S(1)}, u32[]{:S(2)}, u32[]{:S(2)}) collective-permute-start(bf16[512,256]{1,0:T(8,128)(2,1)S(1)} %collective-permute-done.2.refs_0_.refs_3_), channel_id=1, source_target_pairs={{0,8},{8,0},{16,24},{24,16},{32,40},{40,32},{48,56},{56,48},{64,72... | collective-permute-start | bytes 786440 | tf_op jit(solution)/shard_map/ppermute | solution.py:321
  35.8 13.6 %collective-permute-start.11 = (bf16[512,256]{1,0:T(8,128)(2,1)S(1)}, bf16[512,256]{1,0:T(8,128)(2,1)S(1)}, u32[]{:S(2)}, u32[]{:S(2)}) collective-permute-start(bf16[512,256]{1,0:T(8,128)(2,1)S(1)} %collective-permute-done.10.refs_8_), channel_id=1, source_target_pairs={{0,8},{8,0},{16,24},{24,16},{32,40},{40,32},{48,56},{56,48},{64,72... | collective-permute-start | bytes 786440 | tf_op jit(solution)/shard_map/ppermute | solution.py:323
  36.8 6.8 %collective-permute-start.9 = (bf16[256,256]{1,0:T(8,128)(2,1)S(1)}, bf16[256,256]{1,0:T(8,128)(2,1)S(1)}, u32[]{:S(2)}, u32[]{:S(2)}) collective-permute-start(bf16[256,256]{1,0:T(8,128)(2,1)S(1)} %collective-permute-done.8), channel_id=1, source_target_pairs={{32,40},{48,56},{72,64},{88,80},{33,41},{49,57},{73,65},{89,81},{3... | collective-permute-start | bytes 393224 | tf_op jit(solution)/shard_map/ppermute | solution.py:309
  43.7 5.7 %collective-permute-start.7 = (bf16[640,256]{1,0:T(8,128)(2,1)S(1)}, bf16[640,256]{1,0:T(8,128)(2,1)S(1)}, u32[]{:S(2)}, u32[]{:S(2)}) collective-permute-start(bf16[640,256]{1,0:T(8,128)(2,1)S(1)} %collective-permute-done.6.refs_5_), channel_id=1, source_target_pairs={{0,8},{8,0},{16,24},{24,16},{32,40},{40,32},{48,56},{56,48},{64,72... | collective-permute-start | bytes 983048 | tf_op jit(solution)/shard_map/ppermute | solution.py:322

commit v2 on v1

v2 whole, which is shorter than its diff:
```python
import functools

import jax
import jax.numpy as jnp
from jax import lax
from jax.experimental import pallas as pl
from jax.experimental.pallas import tpu as pltpu
from jax.sharding import PartitionSpec as P

HD = 128
GROUP = 8
BLK = 512
PASS = 256
HALF = 128
SCALE = float(HD**-0.5 * 1.4426950408889634)
LOW, HIGH = 2.0**-80, 2.0**100
BF16, F32 = jnp.bfloat16, jnp.float32
NT = (((1,), (1,)), ((), ()))
VMEM_BYTES = 24 * 2**20
SMEM = pl.BlockSpec(memory_space=pltpu.SMEM)
VMEM = pl.BlockSpec(memory_space=pltpu.VMEM)


TOKEN = jax.ShapeDtypeStruct((8, HD), F32)


def cost(units):
    return pl.CostEstimate(
        flops=int(units * 2 * 2 * GROUP * BLK * 256 * 256),
        bytes_accessed=1 << 20,
        transcendentals=int(units * GROUP * BLK * 256),
    )


def params():
    return pltpu.CompilerParams(vmem_limit_bytes=VMEM_BYTES)


def columns(r):
    return slice(r * HD, (r + 1) * HD)


def select_kernel(core_ref, rows_ref, kv_ref, side_ref, out_ref):
    rows = rows_ref[...]
    ids = lax.broadcasted_iota(jnp.int32, (BLK, PASS), 0)
    picked = jnp.where(ids == rows, 1.0, 0.0).astype(BF16)
    out_ref[:PASS] = lax.dot_general(
        picked, kv_ref[...], (((0,), (0,)), ((), ())), preferred_element_type=F32
    ).astype(BF16)

    @pl.when(core_ref[0] == 0)
    def _():
        out_ref[PASS:] = kv_ref[:HALF]

    @pl.when(core_ref[0] != 0)
    def _():
        out_ref[PASS:] = side_ref[HALF : 2 * HALF]


def select(core, rows, kv, side):
    return pl.pallas_call(
        select_kernel,
        out_shape=jax.ShapeDtypeStruct((PASS + HALF, 2 * HD), BF16),
        in_specs=[SMEM, VMEM, VMEM, VMEM],
        out_specs=VMEM,
        compiler_params=params(),
        name="select_rows",
    )(core, rows, kv, side)


def join_kernel(half_ref, mine_ref, peer_ref, out_ref):
    out_ref[:PASS] = mine_ref[:PASS]
    out_ref[PASS : 2 * PASS] = peer_ref[:PASS]

    @pl.when(half_ref[0] == 0)
    def _():
        out_ref[2 * PASS :] = mine_ref[PASS:]

    @pl.when(half_ref[0] != 0)
    def _():
        out_ref[2 * PASS :] = peer_ref[PASS:]


def join(half, mine, peer):
    return pl.pallas_call(
        join_kernel,
        out_shape=jax.ShapeDtypeStruct((2 * PASS + HALF, 2 * HD), BF16),
        in_specs=[SMEM, VMEM, VMEM],
        out_specs=VMEM,
        compiler_params=params(),
        name="join_rows",
    )(half, mine, peer)


def powers(scores):
    return jnp.exp2(scores * SCALE).astype(BF16)


def first_kernel(groups, use_ref, q_ref, kv_ref, *refs):
    near_refs, (acc_ref, token_ref, keys_near, wide) = refs[:-4], refs[-4:]
    token_ref[...] = jnp.zeros_like(token_ref)
    wide[:BLK, :HD] = kv_ref[:, HD:]
    wide[:BLK, HD:] = jnp.ones((BLK, HD), BF16)
    half = BLK // 2
    rows = lax.broadcasted_iota(jnp.int32, (half, half), 0)
    cols = lax.broadcasted_iota(jnp.int32, (half, half), 1)
    causal = cols <= rows
    keys = kv_ref[:, :HD]

    for r in range(GROUP):
        q = q_ref[:, columns(r)]
        scores = lax.dot_general(q, keys[:half], NT, preferred_element_type=F32)
        first = powers(jnp.where(causal, scores[:half], -jnp.inf))
        second = powers(scores[half:])
        scores = lax.dot_general(q[half:], keys[half:], NT, preferred_element_type=F32)
        third = powers(jnp.where(causal, scores, -jnp.inf))
        acc_ref[r, :half] = jnp.dot(first, wide[:half], preferred_element_type=F32)
        acc_ref[r, half:] = jnp.dot(
            jnp.concatenate([second, third], axis=1), wide[:BLK], preferred_element_type=F32
        )

    def put(r, across, total):
        acc_ref[r] = total

    run_groups(groups, use_ref, q_ref, acc_ref, near_refs, keys_near, wide, put)


def first_part(use, q, kv, arrays, groups):
    rows = max(BLK, *[rows_of(case) for _, case, _ in groups])
    return pl.pallas_call(
        functools.partial(first_kernel, groups),
        out_shape=(jax.ShapeDtypeStruct((GROUP, BLK, 2 * HD), F32), TOKEN),
        in_specs=[SMEM] + [VMEM] * (2 + len(arrays)),
        out_specs=(VMEM, VMEM),
        scratch_shapes=[pltpu.VMEM((rows, HD), BF16), pltpu.VMEM((rows, 2 * HD), BF16)],
        compiler_params=params(),
        cost_estimate=cost(4.5),
        name="first_blocks",
    )(use, q, kv, *arrays)


def rows_of(case):
    return sum(stop - start for _, start, stop in case)


def heads(body, unroll):
    if unroll == GROUP:
        for r in range(GROUP):
            body(r, columns(r))
        return

    def step(r, carry):
        body(r, pl.ds(pl.multiple_of(r * HD, HD), HD))
        return carry

    lax.fori_loop(0, GROUP, step, 0, unroll=unroll)


def weighted(case, unroll, q_ref, acc_ref, kv_refs, keys, wide, put):
    at = 0
    for i, start, stop in case:
        end = at + stop - start
        keys[at:end] = kv_refs[i][start:stop, :HD]
        wide[at:end, :HD] = kv_refs[i][start:stop, HD:]
        wide[at:end, HD:] = jnp.ones((end - at, HD), BF16)
        at = end

    def body(r, across):
        scores = lax.dot_general(q_ref[:, across], keys[:at], NT, preferred_element_type=F32)
        put(r, across, acc_ref[r] + jnp.dot(powers(scores), wide[:at], preferred_element_type=F32))

    heads(body, unroll)


def run_groups(groups, use_ref, q_ref, acc_ref, kv_refs, keys, wide, put):
    for flag, case, unroll in groups:

        @pl.when(use_ref[flag] != 0)
        def _():
            weighted(case, unroll, q_ref, acc_ref, kv_refs, keys, wide, put)


def hand_over(use_ref, flag, acc_ref, put):
    @pl.when(use_ref[flag] != 0)
    def _():
        heads(lambda r, across: put(r, across, acc_ref[r]), 1)


def stage_kernel(fresh, more, idle, use_ref, q_ref, *refs):
    kv_refs, (acc_in, acc_ref, token_ref, keys, wide) = refs[:-5], refs[-5:]
    token_ref[...] = jnp.zeros_like(token_ref)

    def put(r, across, total):
        acc_ref[r] = total

    hand_over(use_ref, idle, acc_in, put)
    run_groups(fresh, use_ref, q_ref, acc_in, kv_refs, keys, wide, put)
    run_groups(more, use_ref, q_ref, acc_ref, kv_refs, keys, wide, put)


def stage(use, q, acc, arrays, fresh, more, idle, units):
    rows = max(rows_of(case) for _, case, _ in fresh + more)
    used = sorted({i for _, case, _ in fresh + more for i, _, _ in case})
    fresh, more = (
        [
            (flag, [(used.index(i), start, stop) for i, start, stop in case], unroll)
            for flag, case, unroll in groups
        ]
        for groups in (fresh, more)
    )
    return pl.pallas_call(
        functools.partial(stage_kernel, fresh, more, idle),
        out_shape=(jax.ShapeDtypeStruct(acc.shape, F32), TOKEN),
        in_specs=[SMEM] + [VMEM] * (2 + len(used)),
        out_specs=(VMEM, VMEM),
        scratch_shapes=[pltpu.VMEM((rows, HD), BF16), pltpu.VMEM((rows, 2 * HD), BF16)],
        compiler_params=params(),
        cost_estimate=cost(units),
        name="add_blocks",
    )(use, q, *[arrays[i] for i in used], acc)


def online(q, keys, values, usable, running):
    top, total, mixed = running
    scores = lax.dot_general(q, keys, NT, preferred_element_type=F32) * SCALE
    if usable is not None:
        scores = jnp.where(usable, scores, -jnp.inf)
    fresh = jnp.maximum(top, jnp.max(scores, axis=1, keepdims=True))
    rescale = jnp.exp2(top - fresh)
    weights = jnp.exp2(scores - fresh)
    total = total * rescale + jnp.sum(weights, axis=1, keepdims=True)
    mixed = mixed * rescale + jnp.dot(weights.astype(BF16), values, preferred_element_type=F32)
    return fresh, total, mixed


def final_kernel(earlier, last, idle, use_ref, q_ref, *refs):
    kv_refs, (local_ref, acc_in, out_ref, keys, wide, worst) = refs[:-6], refs[-6:]
    worst[...] = jnp.zeros_like(worst)

    def put(r, across, weighted_sum):
        total = weighted_sum[:, HD:]
        worst[...] = jnp.maximum(
            worst[...], jnp.where((total > LOW) & (total < HIGH), 0.0, 1.0)
        )
        out_ref[:, across] = (weighted_sum[:, :HD] / total).astype(BF16)

    hand_over(use_ref, idle, acc_in, put)
    run_groups(last, use_ref, q_ref, acc_in, kv_refs, keys, wide, put)

    @pl.when(jnp.max(worst[...]) > 0.0)
    def _():
        tile = 128

        def redo(step, carry):
            r, t = step // (BLK // tile), step % (BLK // tile)
            here = pl.ds(pl.multiple_of(t * tile, tile), tile)
            across = pl.ds(pl.multiple_of(r * HD, HD), HD)
            q = q_ref[here, across]
            running = (
                jnp.full((tile, 1), -1e30, F32),
                jnp.zeros((tile, 1), F32),
                jnp.zeros((tile, HD), F32),
            )
            rows = t * tile + lax.broadcasted_iota(jnp.int32, (tile, BLK), 0)
            cols = lax.broadcasted_iota(jnp.int32, (tile, BLK), 1)
            running = online(q, local_ref[:, :HD], local_ref[:, HD:], cols <= rows, running)
            for flag, case, _ in earlier + last:

                def more(state, case=case):
                    for i, start, stop in case:
                        kv = kv_refs[i]
                        state = online(q, kv[start:stop, :HD], kv[start:stop, HD:], None, state)
                    return state

                running = lax.cond(use_ref[flag] != 0, more, lambda state: state, running)
            out_ref[here, across] = (running[2] / running[1]).astype(BF16)
            return carry

        lax.fori_loop(0, GROUP * (BLK // tile), redo, 0)


def final(use, q, acc, local_kv, arrays, earlier, last, idle):
    rows = max(rows_of(case) for _, case, _ in last)
    return pl.pallas_call(
        functools.partial(final_kernel, earlier, last, idle),
        out_shape=jax.ShapeDtypeStruct((BLK, GROUP * HD), BF16),
        in_specs=[SMEM] + [VMEM] * (3 + len(arrays)),
        out_specs=VMEM,
        scratch_shapes=[
            pltpu.VMEM((rows, HD), BF16),
            pltpu.VMEM((rows, 2 * HD), BF16),
            pltpu.VMEM((BLK, HD), F32),
        ],
        compiler_params=params(),
        cost_estimate=cost(4),
        name="last_blocks",
    )(use, q, *arrays, local_kv, acc)


SIBLING = [(s, s ^ 1) for s in range(16)]
PEER = [(s, s ^ 2) for s in range(16)]


def ahead(d, first=0):
    return [(s, s + 4 * d) for s in range(4 * first, 16 - 4 * d)]


def after(messages, token):
    def kernel(*refs):
        del refs

    return pl.pallas_call(
        kernel,
        out_shape=tuple(jax.ShapeDtypeStruct(x.shape, x.dtype) for x in messages),
        in_specs=[VMEM] * (len(messages) + 1),
        out_specs=(VMEM,) * len(messages),
        input_output_aliases={i: i for i in range(len(messages))},
        compiler_params=params(),
        name="hand_on",
    )(*messages, token)


def local(queries, key_states, value_states, passing_rows):
    me = lax.axis_index("seq")
    z, h, c = me // 4, (me // 2) % 2, me % 2
    move = functools.partial(lax.ppermute, axis_name="seq")

    def flags(*conditions):
        return jnp.stack([jnp.asarray(x).astype(jnp.int32) for x in conditions])

    kv_heads = key_states.shape[1] // HD
    rows = key_states.shape[0]
    both = jnp.concatenate(
        [key_states.reshape(rows, kv_heads, HD), value_states.reshape(rows, kv_heads, HD)], axis=2
    ).transpose(1, 0, 2)
    kv = lax.all_to_all(both, "head", split_axis=0, concat_axis=0, tiled=True).reshape(BLK, 2 * HD)

    anchor_side = move(kv[: 2 * HALF], perm=[(0, 1)])
    mine = select(flags(c), passing_rows, kv, anchor_side)
    peer = move(mine, perm=PEER)
    pair = join(flags(h), mine, peer)
    one = move(pair, perm=ahead(1))
    three = move(pair, perm=ahead(3))
    pair_side = move(pair, perm=SIBLING)

    def both(i):
        return ((i, 0, 2 * PASS), (i + 1, 0, 2 * PASS))

    def anchor(i):
        return ((i, 2 * PASS, 2 * PASS + HALF), (i + 1, 2 * PASS, 2 * PASS + HALF))

    arrays = [pair, pair_side] + [None] * 6
    near = (
        (0, ((0, PASS, 2 * PASS), (1, PASS, 2 * PASS)), GROUP),
        (1, ((1, 0, PASS),), GROUP),
        (2, anchor(0), 1),
    )
    fresh = ((3, both(2), GROUP),)
    more = ((4, anchor(2), 1), (5, both(4) + anchor(4), GROUP))
    last = ((6, both(6) + anchor(6), 2), (5, both(6), GROUP))
    use = flags(
        h == 1, c == 1, (z == 0) & (me > 0), z >= 1, z == 1, z == 3, z == 2, z == 0, z < 2
    )
    q = queries

    acc, token = first_part(use, q, kv, arrays[:2], near)
    (one,) = after((one,), token)
    (three,) = after((three,), token)
    two = move(one, perm=ahead(1, 1))
    arrays[2], arrays[3] = one, move(one, perm=SIBLING)
    arrays[4], arrays[5] = three, move(three, perm=SIBLING)
    acc, token = stage(use, q, acc, arrays, fresh, more, 7, 9)
    (two,) = after((two,), token)
    arrays[6], arrays[7] = two, move(two, perm=SIBLING)
    return final(use, q, acc, kv, arrays, near + fresh + more, last, 8)


def solution(mesh):
    in_specs = (
        P("seq", "head"),
        P(("seq", "head"), None),
        P(("seq", "head"), None),
        P("head", "seq"),
    )
    return jax.shard_map(
        local, mesh=mesh, in_specs=in_specs, out_specs=P("seq", "head"), check_vma=False
    )
```

time: 182 us -> 183 us (level)
  waiting for transfers between devices: 7.17 us -> 9.46 us
    ppermute x1, waiting for transfers between devices: 0.01 us -> 5.67 us  [local(): peer = move(mine, perm=PEER)]
    ppermute x1, waiting for transfers between devices: 5.14 us -> 0.01 us  [local(): one = move(pair, perm=ahead(1))]
    ppermute x9 -> x6, starting transfers between devices: 7.06 us -> 4.61 us  [the longest x1 1.29 us: local(): three = move(pair, perm=ahead(3))]
    ppermute x9 -> x6, waiting for transfers between devices: 2.02 us -> 3.78 us  [the longest x1 2.18 us: local(): three = move(pair, perm=ahead(3))]
    pallas_call x5 -> x8, Pallas kernels: 148 us -> 149 us  [the longest x1 131 us: final(): pl.pallas_call(functools.partial(final_kernel, earlier, last, idle), out_...]
  transfers between devices with their start and end apart: 12 -> 9, of which waited for: 2 -> 4; matrix products, arithmetic and copies ran while one was open for 0% -> 0% of each run, Pallas kernels for 9% -> 10%
where the time goes in v2:
time: 183 us; the launch traced here: 182 us
  Pallas kernels  149 us (81%)
  blocking collectives  10.8 us (6%)
  starting transfers between devices  9.5 us (5%)
  waiting for transfers between devices  9.46 us (5%)
  local copies, waits for them, and re-layouts  3.88 us (2%)
    pallas_call x1, Pallas kernels, final(): pl.pallas_call(functools.partial(final_kernel, earlier, last, idle), out_...  131 us
    pallas_call x1, Pallas kernels, stage(): pl.pallas_call(functools.partial(stage_kernel, fresh, more, idle), out_sh...  11.3 us
    all_to_all x1, blocking collectives, local(): lax.all_to_all(both, 'head', split_axis=0, concat_axis=0, tiled=True)  10.8 us
    pallas_call x1, Pallas kernels, first_part(): pl.pallas_call(functools.partial(first_kernel, groups), out_shape=(jax.Sh...  6.37 us
    ppermute x1, waiting for transfers between devices, local(): peer = move(mine, perm=PEER)  5.67 us
  transfers between devices with their start and end apart: 9, of which 4 were waited for; matrix products, arithmetic and copies ran while one was open for 0% of the time, Pallas kernels for 10%

profile of v2, /device:TPU:113, one launch (start us, length us, event | category | flops | bytes accessed | tf_op | source)
XLA Modules:
  0.0 182.5 jit_solution(5641613098373173102)
XLA Ops:
  0.0 0.0 copy-start
  0.0 0.9 copy-done
  0.9 1.0 copy_bitcast_fusion
  1.9 10.8 %all_to_all.5 = bf16[8,64,256]{2,1,0:T(8,128)(2,1)S(1)} all-to-all(bf16[8,64,256]{2,1,0:T(8,128)(2,1)S(1)} %maximum_bitcast_fusion), channel_id=1, replica_groups=mesh['seq'=16,'head'=8] {'head'}, dimensions={0} | all-to-all | bytes 524288 | tf_op jit(solution)/shard_map/all_to_all | solution.py:336
  12.8 0.7 collective-permute-start
  13.4 0.0 collective-permute-done.side_ref
  13.5 0.0 copy-start.1
  13.5 0.7 copy-done.1
  14.1 0.3 select_rows.1.mine_ref
  14.4 0.4 collective-permute-start.1
  14.9 5.7 %collective-permute-done.1.peer_ref = bf16[384,256]{1,0:T(8,128)(2,1)S(1)} collective-permute-done((bf16[384,256]{1,0:T(8,128)(2,1)S(1)}, bf16[384,256]{1,0:T(8,128)(2,1)S(1)}, u32[]{:S(2)}, u32[]{:S(2)}) %collective-permute-start.1) | collective-permute-done | bytes 196640 | tf_op jit(solution)/shard_map/ppermute | solution.py:340
  20.6 3.2 %collective-permute-start.2 = (bf16[640,256]{1,0:T(8,128)(2,1)S(1)}, bf16[640,256]{1,0:T(8,128)(2,1)S(1)}, u32[]{:S(2)}, u32[]{:S(2)}) collective-permute-start(bf16[640,256]{1,0:T(8,128)(2,1)S(1)} %join_rows.1.refs_0_), channel_id=1, source_target_pairs={{0,8},{8,0},{16,24},{24,16},{32,40},{40,32},{48,56},{56,48},{64,72... | collective-permute-start | bytes 983048 | tf_op jit(solution)/shard_map/ppermute | solution.py:344
  23.7 0.1 stack.56
  23.9 1.3 collective-permute-start.5
  25.1 1.3 collective-permute-start.3
  26.4 0.0 collective-permute-done.2.refs_1_
  26.5 0.0 copy-start.2
  26.5 1.2 copy-done.2
  27.7 0.0 copy-start.3
  27.7 6.4 %first_blocks.1 = (f32[8,512,256]{2,1,0:T(8,128)S(1)}, f32[8,128]{1,0:T(8,128)S(1)}) custom-call(s32[9]{0:T(128)S(1)} %stack.57.use_ref, bf16[512,1024]{1,0:T(8,128)(2,1)S(1)} %copy-done.2, bf16[512,256]{1,0:T(8,128)(2,1)S(1)} %bitcast.26, bf16[640,256]{1,0:T(8,128)(2,1)S(1)} %join_rows.1.refs_0_, bf16[640,256]{1,0:T(8,128)(2,1)S(1)} %collective-permute-done.2.refs_1_), custom_call_target="tpu_custom_call" | custom-call | flops 4831838208 | bytes 1048576 | tf_op jit(solution)/shard_map/first_blocks/pallas_call | solution.py:130
  34.1 2.2 %collective-permute-done.5.refs_0_ = bf16[640,256]{1,0:T(8,128)(2,1)S(1)} collective-permute-done((bf16[640,256]{1,0:T(8,128)(2,1)S(1)}, bf16[640,256]{1,0:T(8,128)(2,1)S(1)}, u32[]{:S(2)}, u32[]{:S(2)}) %collective-permute-start.5) | collective-permute-done | bytes 327712 | tf_op jit(solution)/shard_map/ppermute | solution.py:343
  36.2 0.8 collective-permute-start.6
  37.1 0.0 collective-permute-done.3.refs_0_
  37.1 0.1 collective-permute-start.4
  37.2 1.3 collective-permute-start.7
  38.5 0.0 collective-permute-done.6.refs_3_.refs_5_
  38.5 0.3 collective-permute-done.4.refs_1_.refs_3_
  38.8 0.0 copy-done.3
  38.8 11.3 %add_blocks.1 = (f32[8,512,256]{2,1,0:T(8,128)S(1)}, f32[8,128]{1,0:T(8,128)S(1)}) custom-call(s32[9]{0:T(128)S(1)} %stack.57.use_ref, bf16[512,1024]{1,0:T(8,128)(2,1)S(1)} %copy-done.3, bf16[640,256]{1,0:T(8,128)(2,1)S(1)} %hand_on.3.refs_0_.refs_2_, bf16[640,256]{1,0:T(8,128)(2,1)S(1)} %collective-permute-done.4.refs_1_.refs_3_, ...), custom_call_target="tpu_custom_call" | custom-call | flops 9663676416 | bytes 1048576 | tf_op jit(solution)/shard_map/add_blocks/pallas_call | solution.py:211
  50.1 0.0 collective-permute-done.7.refs_0_
  50.1 0.5 collective-permute-start.8
  50.6 1.3 collective-permute-done.8.refs_7_
  51.8 130.6 %last_blocks.1 = bf16[512,1024]{1,0:T(8,128)(2,1)} custom-call(s32[9]{0:T(128)S(1)} %stack.57.use_ref, bf16[512,1024]{1,0:T(8,128)(2,1)S(1)} %copy-done.3, bf16[640,256]{1,0:T(8,128)(2,1)S(1)} %join_rows.1.refs_0_, bf16[640,256]{1,0:T(8,128)(2,1)S(1)} %collective-permute-done.2.refs_1_, bf16[640,256]{1,0:T(8,128)(2,1)S(1)} %hand_on.3.refs_0_.refs_2_, ...), custom_call_target="tpu_custom_call" | custom-call | flops 4294967296 | bytes 1048576 | tf_op jit(solution)/shard_map/last_blocks/pallas_call | solution.py:284
  (7 shorter events, 0.1 us)
Async XLA Ops:
  0.0 0.9 copy-start
  12.8 0.7 collective-permute-start
  13.5 0.7 copy-start.1
  14.4 6.1 %collective-permute-start.1 = (bf16[384,256]{1,0:T(8,128)(2,1)S(1)}, bf16[384,256]{1,0:T(8,128)(2,1)S(1)}, u32[]{:S(2)}, u32[]{:S(2)}) collective-permute-start(bf16[384,256]{1,0:T(8,128)(2,1)S(1)} %select_rows.1.mine_ref), channel_id=1, source_target_pairs={{0,16},{8,24},{16,0},{24,8},{32,48},{40,56},{48,32},{56,40},{64,80... | collective-permute-start | bytes 589832 | tf_op jit(solution)/shard_map/ppermute | solution.py:340
  20.6 5.9 %collective-permute-start.2 = (bf16[640,256]{1,0:T(8,128)(2,1)S(1)}, bf16[640,256]{1,0:T(8,128)(2,1)S(1)}, u32[]{:S(2)}, u32[]{:S(2)}) collective-permute-start(bf16[640,256]{1,0:T(8,128)(2,1)S(1)} %join_rows.1.refs_0_), channel_id=1, source_target_pairs={{0,8},{8,0},{16,24},{24,16},{32,40},{40,32},{48,56},{56,48},{64,72... | collective-permute-start | bytes 983048 | tf_op jit(solution)/shard_map/ppermute | solution.py:344
  23.9 12.4 %collective-permute-start.5 = (bf16[640,256]{1,0:T(8,128)(2,1)S(1)}, bf16[640,256]{1,0:T(8,128)(2,1)S(1)}, u32[]{:S(2)}, u32[]{:S(2)}) collective-permute-start(bf16[640,256]{1,0:T(8,128)(2,1)S(1)} %join_rows.1.refs_0_), channel_id=1, source_target_pairs={{0,96},{8,104},{16,112},{24,120},{1,97},{9,105},{17,113},{25,121},... | collective-permute-start | bytes 983048 | tf_op jit(solution)/shard_map/ppermute | solution.py:343
  25.1 11.9 %collective-permute-start.3 = (bf16[640,256]{1,0:T(8,128)(2,1)S(1)}, bf16[640,256]{1,0:T(8,128)(2,1)S(1)}, u32[]{:S(2)}, u32[]{:S(2)}) collective-permute-start(bf16[640,256]{1,0:T(8,128)(2,1)S(1)} %join_rows.1.refs_0_), channel_id=1, source_target_pairs={{0,32},{8,40},{16,48},{24,56},{32,64},{40,72},{48,80},{56,88},{64,... | collective-permute-start | bytes 983048 | tf_op jit(solution)/shard_map/ppermute | solution.py:342
  26.5 1.2 copy-start.2
  27.7 11.1 %copy-start.3 = (bf16[512,1024]{1,0:T(8,128)(2,1)S(1)}, bf16[512,1024]{1,0:T(8,128)(2,1)}, u32[]{:S(2)}) copy-start(bf16[512,1024]{1,0:T(8,128)(2,1)} %q_ref.5) | copy-start | bytes 3145732
  36.2 2.2 %collective-permute-start.6 = (bf16[640,256]{1,0:T(8,128)(2,1)S(1)}, bf16[640,256]{1,0:T(8,128)(2,1)S(1)}, u32[]{:S(2)}, u32[]{:S(2)}) collective-permute-start(bf16[640,256]{1,0:T(8,128)(2,1)S(1)} %hand_on.4.refs_2_.refs_4_), channel_id=1, source_target_pairs={{0,8},{8,0},{16,24},{24,16},{32,40},{40,32},{48,56},{56,48},{64,72... | collective-permute-start | bytes 983048 | tf_op jit(solution)/shard_map/ppermute | solution.py:371
  37.1 1.7 collective-permute-start.4
  37.2 12.9 %collective-permute-start.7 = (bf16[640,256]{1,0:T(8,128)(2,1)S(1)}, bf16[640,256]{1,0:T(8,128)(2,1)S(1)}, u32[]{:S(2)}, u32[]{:S(2)}) collective-permute-start(bf16[640,256]{1,0:T(8,128)(2,1)S(1)} %hand_on.3.refs_0_.refs_2_), channel_id=1, source_target_pairs={{32,64},{40,72},{48,80},{56,88},{64,96},{72,104},{80,112},{88,120}... | collective-permute-start | bytes 983048 | tf_op jit(solution)/shard_map/ppermute | solution.py:369
  50.1 1.7 collective-permute-start.8

commit v3 on v2

--- a/solution.py
+++ b/solution.py
@@ -12,6 +12,7 @@
 BLK = 512
 PASS = 256
 HALF = 128
+SIDE = 4
 SCALE = float(HD**-0.5 * 1.4426950408889634)
 LOW, HIGH = 2.0**-80, 2.0**100
 BF16, F32 = jnp.bfloat16, jnp.float32
@@ -40,56 +41,59 @@
     return slice(r * HD, (r + 1) * HD)
 
 
-def select_kernel(core_ref, rows_ref, kv_ref, side_ref, out_ref):
+def select_kernel(core_ref, rows_ref, kv_ref, side_ref, out_ref, half_ref):
     rows = rows_ref[...]
     ids = lax.broadcasted_iota(jnp.int32, (BLK, PASS), 0)
     picked = jnp.where(ids == rows, 1.0, 0.0).astype(BF16)
-    out_ref[:PASS] = lax.dot_general(
+    out_ref[...] = lax.dot_general(
         picked, kv_ref[...], (((0,), (0,)), ((), ())), preferred_element_type=F32
     ).astype(BF16)
 
     @pl.when(core_ref[0] == 0)
     def _():
-        out_ref[PASS:] = kv_ref[:HALF]
+        half_ref[...] = kv_ref[:HALF]
 
     @pl.when(core_ref[0] != 0)
     def _():
-        out_ref[PASS:] = side_ref[HALF : 2 * HALF]
+        half_ref[...] = side_ref[HALF : 2 * HALF]
 
 
 def select(core, rows, kv, side):
     return pl.pallas_call(
         select_kernel,
-        out_shape=jax.ShapeDtypeStruct((PASS + HALF, 2 * HD), BF16),
+        out_shape=(
+            jax.ShapeDtypeStruct((PASS, 2 * HD), BF16),
+            jax.ShapeDtypeStruct((HALF, 2 * HD), BF16),
+        ),
         in_specs=[SMEM, VMEM, VMEM, VMEM],
-        out_specs=VMEM,
+        out_specs=(VMEM, VMEM),
         compiler_params=params(),
         name="select_rows",
     )(core, rows, kv, side)
 
 
-def join_kernel(half_ref, mine_ref, peer_ref, out_ref):
-    out_ref[:PASS] = mine_ref[:PASS]
-    out_ref[PASS : 2 * PASS] = peer_ref[:PASS]
-
-    @pl.when(half_ref[0] == 0)
-    def _():
-        out_ref[2 * PASS :] = mine_ref[PASS:]
-
-    @pl.when(half_ref[0] != 0)
-    def _():
-        out_ref[2 * PASS :] = peer_ref[PASS:]
-
-
-def join(half, mine, peer):
+def join_kernel(where_ref, mine_ref, peer_ref, half_ref, peer_half_ref, out_ref):
+    out_ref[:PASS] = mine_ref[...]
+    out_ref[PASS : 2 * PASS] = peer_ref[...]
+
+    @pl.when(where_ref[0] == 0)
+    def _():
+        out_ref[2 * PASS :] = half_ref[...]
+
+    @pl.when(where_ref[0] != 0)
+    def _():
+        out_ref[2 * PASS :] = peer_half_ref[...]
+
+
+def join(where, mine, peer, half, peer_half):
     return pl.pallas_call(
         join_kernel,
         out_shape=jax.ShapeDtypeStruct((2 * PASS + HALF, 2 * HD), BF16),
-        in_specs=[SMEM, VMEM, VMEM],
+        in_specs=[SMEM, VMEM, VMEM, VMEM, VMEM],
         out_specs=VMEM,
         compiler_params=params(),
         name="join_rows",
-    )(half, mine, peer)
+    )(where, mine, peer, half, peer_half)
 
 
 def powers(scores):
@@ -134,7 +138,7 @@
         out_specs=(VMEM, VMEM),
         scratch_shapes=[pltpu.VMEM((rows, HD), BF16), pltpu.VMEM((rows, 2 * HD), BF16)],
         compiler_params=params(),
-        cost_estimate=cost(4.5),
+        cost_estimate=cost(2.5),
         name="first_blocks",
     )(use, q, kv, *arrays)
 
@@ -234,8 +238,13 @@
 
 
 def final_kernel(earlier, last, idle, use_ref, q_ref, *refs):
-    kv_refs, (local_ref, acc_in, out_ref, keys, wide, worst) = refs[:-6], refs[-6:]
+    kv_refs, (local_ref, acc_in, result_ref, keys, wide, worst, out_ref, sems) = refs[:-8], refs[-8:]
     worst[...] = jnp.zeros_like(worst)
+
+    def send(r, across):
+        return pltpu.make_async_copy(
+            out_ref.at[:, across], result_ref.at[:, across], sems.at[r]
+        )
 
     def put(r, across, weighted_sum):
         total = weighted_sum[:, HD:]
@@ -243,9 +252,13 @@
             worst[...], jnp.where((total > LOW) & (total < HIGH), 0.0, 1.0)
         )
         out_ref[:, across] = (weighted_sum[:, :HD] / total).astype(BF16)
+        send(r, across).start()
 
     hand_over(use_ref, idle, acc_in, put)
     run_groups(last, use_ref, q_ref, acc_in, kv_refs, keys, wide, put)
+
+    for r in range(GROUP):
+        send(r, columns(r)).wait()
 
     @pl.when(jnp.max(worst[...]) > 0.0)
     def _():
@@ -277,6 +290,7 @@
             return carry
 
         lax.fori_loop(0, GROUP * (BLK // tile), redo, 0)
+        pltpu.sync_copy(out_ref, result_ref)
 
 
 def final(use, q, acc, local_kv, arrays, earlier, last, idle):
@@ -285,11 +299,13 @@
         functools.partial(final_kernel, earlier, last, idle),
         out_shape=jax.ShapeDtypeStruct((BLK, GROUP * HD), BF16),
         in_specs=[SMEM] + [VMEM] * (3 + len(arrays)),
-        out_specs=VMEM,
+        out_specs=pl.BlockSpec(memory_space=pl.ANY),
         scratch_shapes=[
             pltpu.VMEM((rows, HD), BF16),
             pltpu.VMEM((rows, 2 * HD), BF16),
             pltpu.VMEM((BLK, HD), F32),
+            pltpu.VMEM((BLK, GROUP * HD), BF16),
+            pltpu.SemaphoreType.DMA((GROUP,)),
         ],
         compiler_params=params(),
         cost_estimate=cost(4),
@@ -336,12 +352,12 @@
     kv = lax.all_to_all(both, "head", split_axis=0, concat_axis=0, tiled=True).reshape(BLK, 2 * HD)
 
     anchor_side = move(kv[: 2 * HALF], perm=[(0, 1)])
-    mine = select(flags(c), passing_rows, kv, anchor_side)
+    mine, half = select(flags(c), passing_rows, kv, anchor_side)
     peer = move(mine, perm=PEER)
-    pair = join(flags(h), mine, peer)
+    peer_half = move(half, perm=[(0, 2), (1, 3)])
+    pair = join(flags(h), mine, peer, half, peer_half)
     one = move(pair, perm=ahead(1))
     three = move(pair, perm=ahead(3))
-    pair_side = move(pair, perm=SIBLING)
 
     def both(i):
         return ((i, 0, 2 * PASS), (i + 1, 0, 2 * PASS))
@@ -349,30 +365,36 @@
     def anchor(i):
         return ((i, 2 * PASS, 2 * PASS + HALF), (i + 1, 2 * PASS, 2 * PASS + HALF))
 
-    arrays = [pair, pair_side] + [None] * 6
-    near = (
-        (0, ((0, PASS, 2 * PASS), (1, PASS, 2 * PASS)), GROUP),
-        (1, ((1, 0, PASS),), GROUP),
-        (2, anchor(0), 1),
-    )
-    fresh = ((3, both(2), GROUP),)
-    more = ((4, anchor(2), 1), (5, both(4) + anchor(4), GROUP))
-    last = ((6, both(6) + anchor(6), 2), (5, both(6), GROUP))
+    arrays = [pair] + [None] * 7
+    near = ((0, ((0, PASS, 2 * PASS),), GROUP),)
+    fresh = ((1, both(2), GROUP),)
+    more = ((2, anchor(2), 1), (3, both(4) + anchor(4), GROUP))
+    side = (
+        (4, ((1, 0, 2 * PASS),), GROUP),
+        (5, ((1, 0, PASS),), SIDE),
+        (6, ((1, PASS, 2 * PASS),), SIDE),
+    )
+    side_more = ((7, anchor(0), 1),)
+    last = ((8, both(6) + anchor(6), 4), (3, both(6), GROUP))
     use = flags(
-        h == 1, c == 1, (z == 0) & (me > 0), z >= 1, z == 1, z == 3, z == 2, z == 0, z < 2
+        h == 1, z >= 1, z == 1, z == 3,
+        (h == 1) & (c == 1), (h == 0) & (c == 1), (h == 1) & (c == 0),
+        (z == 0) & (me > 0), z == 2, z == 0, h + c == 0, z < 2,
     )
     q = queries
 
-    acc, token = first_part(use, q, kv, arrays[:2], near)
+    acc, token = first_part(use, q, kv, arrays[:1], near)
     (one,) = after((one,), token)
     (three,) = after((three,), token)
+    arrays[1] = move(after((pair,), token)[0], perm=SIBLING)
     two = move(one, perm=ahead(1, 1))
     arrays[2], arrays[3] = one, move(one, perm=SIBLING)
     arrays[4], arrays[5] = three, move(three, perm=SIBLING)
-    acc, token = stage(use, q, acc, arrays, fresh, more, 7, 9)
+    acc, token = stage(use, q, acc, arrays, fresh, more, 9, 9)
     (two,) = after((two,), token)
     arrays[6], arrays[7] = two, move(two, perm=SIBLING)
-    return final(use, q, acc, kv, arrays, near + fresh + more, last, 8)
+    acc, _ = stage(use, q, acc, arrays, side, side_more, 10, 2)
+    return final(use, q, acc, kv, arrays, near + fresh + more + side + side_more, last, 11)
 
 
 def solution(mesh):

time: 183 us -> 177 us (0.967)
  Pallas kernels: 149 us -> 145 us
  waiting for transfers between devices: 9.46 us -> 6.72 us
    pallas_call x1, Pallas kernels: 131 us -> 126 us  [final(): pl.pallas_call(functools.partial(final_kernel, earlier, last, idle), out_...]
    pallas_call x1 -> x2, Pallas kernels: 11.3 us -> 15 us  [stage(): pl.pallas_call(functools.partial(stage_kernel, fresh, more, idle), out_sh...]
    ppermute x1, starting transfers between devices: 0.83 us -> 3.49 us  [local(): arrays[4], arrays[5] = (three, move(three, perm=SIBLING))]
    pallas_call x1, Pallas kernels: 6.37 us -> 3.83 us  [first_part(): pl.pallas_call(functools.partial(first_kernel, groups), out_shape=(jax.Sh...]
    ppermute x1 -> x2, starting transfers between devices: 3.18 us -> 1.16 us  [the longest x1 0.65 us: local(): peer_half = move(half, perm=[(0, 2), (1, 3)])]
  transfers between devices with their start and end apart: 9 -> 10, of which waited for: 4 -> 2; matrix products, arithmetic and copies ran while one was open for 0% -> 0% of each run, Pallas kernels for 10% -> 11%
where the time goes in v3:
time: 177 us
  Pallas kernels  145 us (82%)
  blocking collectives  10.8 us (6%)
  starting transfers between devices  9.93 us (6%)
  waiting for transfers between devices  6.72 us (4%)
  local copies, waits for them, and re-layouts  3.91 us (2%)
    pallas_call x1, Pallas kernels, final(): pl.pallas_call(functools.partial(final_kernel, earlier, last, idle), out_...  126 us
    pallas_call x2, Pallas kernels, stage(): pl.pallas_call(functools.partial(stage_kernel, fresh, more, idle), out_sh...  15 us
    all_to_all x1, blocking collectives, local(): lax.all_to_all(both, 'head', split_axis=0, concat_axis=0, tiled=True)  10.8 us
    ppermute x1, waiting for transfers between devices, local(): peer = move(mine, perm=PEER)  4.27 us
    pallas_call x1, Pallas kernels, first_part(): pl.pallas_call(functools.partial(first_kernel, groups), out_shape=(jax.Sh...  3.83 us
  transfers between devices with their start and end apart: 10, of which 2 were waited for; matrix products, arithmetic and copies ran while one was open for 0% of the time, Pallas kernels for 11%

profile of v3, /device:TPU:113, one launch (start us, length us, event | category | flops | bytes accessed | tf_op | source)
XLA Modules:
  0.0 176.8 jit_solution(15620263569468545914)
XLA Ops:
  0.0 0.0 copy-start
  0.0 0.9 copy-done
  0.9 1.0 copy_bitcast_fusion
  1.9 10.8 %all_to_all.5 = bf16[8,64,256]{2,1,0:T(8,128)(2,1)S(1)} all-to-all(bf16[8,64,256]{2,1,0:T(8,128)(2,1)S(1)} %maximum_bitcast_fusion), channel_id=1, replica_groups=mesh['seq'=16,'head'=8] {'head'}, dimensions={0} | all-to-all | bytes 524288 | tf_op jit(solution)/shard_map/all_to_all | solution.py:352
  12.8 0.7 collective-permute-start
  13.4 0.0 collective-permute-done.side_ref
  13.5 0.0 copy-start.1
  13.5 0.7 copy-done.1
  14.1 0.3 select_rows.1
  14.4 0.4 collective-permute-start.1
  14.9 0.7 collective-permute-start.2
  15.5 0.0 collective-permute-done.2.peer_half_ref
  15.6 4.3 %collective-permute-done.1.peer_ref = bf16[256,256]{1,0:T(8,128)(2,1)S(1)} collective-permute-done((bf16[256,256]{1,0:T(8,128)(2,1)S(1)}, bf16[256,256]{1,0:T(8,128)(2,1)S(1)}, u32[]{:S(2)}, u32[]{:S(2)}) %collective-permute-start.1) | collective-permute-done | bytes 131104 | tf_op jit(solution)/shard_map/ppermute | solution.py:356
  19.9 1.3 collective-permute-start.6
  21.2 1.3 collective-permute-start.4
  22.5 0.1 stack.71
  22.6 0.0 copy-start.2
  22.6 1.2 copy-done.2
  23.8 0.0 copy-start.3
  23.9 3.8 %first_blocks.1 = (f32[8,512,256]{2,1,0:T(8,128)S(1)}, f32[8,128]{1,0:T(8,128)S(1)}) custom-call(s32[12]{0:T(128)S(1)} %stack.72.use_ref, bf16[512,1024]{1,0:T(8,128)(2,1)S(1)} %copy-done.2, bf16[512,256]{1,0:T(8,128)(2,1)S(1)} %bitcast.29, bf16[640,256]{1,0:T(8,128)(2,1)S(1)} %join_rows.1.refs_0_), custom_call_target="tpu_custom_call" | custom-call | flops 2684354560 | bytes 1048576 | tf_op jit(solution)/shard_map/first_blocks/pallas_call | solution.py:134
  27.7 2.4 %collective-permute-done.6.refs_0_ = bf16[640,256]{1,0:T(8,128)(2,1)S(1)} collective-permute-done((bf16[640,256]{1,0:T(8,128)(2,1)S(1)}, bf16[640,256]{1,0:T(8,128)(2,1)S(1)}, u32[]{:S(2)}, u32[]{:S(2)}) %collective-permute-start.6) | collective-permute-done | bytes 327712 | tf_op jit(solution)/shard_map/ppermute | solution.py:360
  30.1 3.5 %collective-permute-start.7 = (bf16[640,256]{1,0:T(8,128)(2,1)S(1)}, bf16[640,256]{1,0:T(8,128)(2,1)S(1)}, u32[]{:S(2)}, u32[]{:S(2)}) collective-permute-start(bf16[640,256]{1,0:T(8,128)(2,1)S(1)} %hand_on.6.refs_2_.refs_4_), channel_id=1, source_target_pairs={{0,8},{8,0},{16,24},{24,16},{32,40},{40,32},{48,56},{56,48},{64,72... | collective-permute-start | bytes 983048 | tf_op jit(solution)/shard_map/ppermute | solution.py:392
  33.6 0.0 collective-permute-done.4.refs_0_
  33.6 0.1 collective-permute-start.5
  33.7 0.5 collective-permute-start.3
  34.2 1.3 collective-permute-start.8
  35.5 0.0 collective-permute-done.7.refs_3_.refs_5_
  35.5 0.0 collective-permute-done.5.refs_1_.refs_3_
  35.6 0.0 copy-done.3
  35.6 11.3 %add_blocks.2 = (f32[8,512,256]{2,1,0:T(8,128)S(1)}, f32[8,128]{1,0:T(8,128)S(1)}) custom-call(s32[12]{0:T(128)S(1)} %stack.72.use_ref, bf16[512,1024]{1,0:T(8,128)(2,1)S(1)} %copy-done.3, bf16[640,256]{1,0:T(8,128)(2,1)S(1)} %hand_on.5.refs_0_.refs_2_, bf16[640,256]{1,0:T(8,128)(2,1)S(1)} %collective-permute-done.5.refs_1_.refs_3_, ...), custom_call_target="tpu_custom_call" | custom-call | flops 9663676416 | bytes 1048576 | tf_op jit(solution)/shard_map/add_blocks/pallas_call | solution.py:215
  46.9 0.0 collective-permute-done.8.refs_0_
  46.9 0.2 collective-permute-start.9
  47.1 0.0 collective-permute-done.3.refs_1_
  47.1 3.7 %add_blocks.3 = (f32[8,512,256]{2,1,0:T(8,128)S(1)}, f32[8,128]{1,0:T(8,128)}) custom-call(s32[12]{0:T(128)S(1)} %stack.72.use_ref, bf16[512,1024]{1,0:T(8,128)(2,1)S(1)} %copy-done.3, bf16[640,256]{1,0:T(8,128)(2,1)S(1)} %join_rows.1.refs_0_, bf16[640,256]{1,0:T(8,128)(2,1)S(1)} %collective-permute-done.3.refs_1_, f32[8,512,256]{2,1,0:T(8,128)S(1)} %get-tuple-element.17.refs_2_), custom_call_target="tpu_custom_call" | custom-call | flops 2147483648 | bytes 1048576 | tf_op jit(solution)/shard_map/add_blocks/pallas_call | solution.py:215
  50.8 0.0 collective-permute-done.9.refs_7_
  50.8 125.8 %last_blocks.1 = bf16[512,1024]{1,0:T(8,128)(2,1)} custom-call(s32[12]{0:T(128)S(1)} %stack.72.use_ref, bf16[512,1024]{1,0:T(8,128)(2,1)S(1)} %copy-done.3, bf16[640,256]{1,0:T(8,128)(2,1)S(1)} %join_rows.1.refs_0_, bf16[640,256]{1,0:T(8,128)(2,1)S(1)} %collective-permute-done.3.refs_1_, bf16[640,256]{1,0:T(8,128)(2,1)S(1)} %hand_on.5.refs_0_.refs_2_, ...), custom_call_target="tpu_custom_call" | custom-call | flops 4294967296 | bytes 1048576 | tf_op jit(solution)/shard_map/last_blocks/pallas_call | solution.py:298
  (9 shorter events, 0.1 us)
Async XLA Ops:
  0.0 0.9 copy-start
  12.8 0.7 collective-permute-start
  13.5 0.7 copy-start.1
  14.4 5.4 %collective-permute-start.1 = (bf16[256,256]{1,0:T(8,128)(2,1)S(1)}, bf16[256,256]{1,0:T(8,128)(2,1)S(1)}, u32[]{:S(2)}, u32[]{:S(2)}) collective-permute-start(bf16[256,256]{1,0:T(8,128)(2,1)S(1)} %get-tuple-element.12.mine_ref), channel_id=1, source_target_pairs={{0,16},{8,24},{16,0},{24,8},{32,48},{40,56},{48,32},{56,40},{64,80... | collective-permute-start | bytes 393224 | tf_op jit(solution)/shard_map/ppermute | solution.py:356
  14.9 0.7 collective-permute-start.2
  19.9 10.3 %collective-permute-start.6 = (bf16[640,256]{1,0:T(8,128)(2,1)S(1)}, bf16[640,256]{1,0:T(8,128)(2,1)S(1)}, u32[]{:S(2)}, u32[]{:S(2)}) collective-permute-start(bf16[640,256]{1,0:T(8,128)(2,1)S(1)} %join_rows.1.refs_0_), channel_id=1, source_target_pairs={{0,96},{8,104},{16,112},{24,120},{1,97},{9,105},{17,113},{25,121},... | collective-permute-start | bytes 983048 | tf_op jit(solution)/shard_map/ppermute | solution.py:360
  21.2 12.5 %collective-permute-start.4 = (bf16[640,256]{1,0:T(8,128)(2,1)S(1)}, bf16[640,256]{1,0:T(8,128)(2,1)S(1)}, u32[]{:S(2)}, u32[]{:S(2)}) collective-permute-start(bf16[640,256]{1,0:T(8,128)(2,1)S(1)} %join_rows.1.refs_0_), channel_id=1, source_target_pairs={{0,32},{8,40},{16,48},{24,56},{32,64},{40,72},{48,80},{56,88},{64,... | collective-permute-start | bytes 983048 | tf_op jit(solution)/shard_map/ppermute | solution.py:359
  22.6 1.2 copy-start.2
  23.8 11.7 %copy-start.3 = (bf16[512,1024]{1,0:T(8,128)(2,1)S(1)}, bf16[512,1024]{1,0:T(8,128)(2,1)}, u32[]{:S(2)}) copy-start(bf16[512,1024]{1,0:T(8,128)(2,1)} %q_ref.7) | copy-start | bytes 3145732
  30.1 5.4 %collective-permute-start.7 = (bf16[640,256]{1,0:T(8,128)(2,1)S(1)}, bf16[640,256]{1,0:T(8,128)(2,1)S(1)}, u32[]{:S(2)}, u32[]{:S(2)}) collective-permute-start(bf16[640,256]{1,0:T(8,128)(2,1)S(1)} %hand_on.6.refs_2_.refs_4_), channel_id=1, source_target_pairs={{0,8},{8,0},{16,24},{24,16},{32,40},{40,32},{48,56},{56,48},{64,72... | collective-permute-start | bytes 983048 | tf_op jit(solution)/shard_map/ppermute | solution.py:392
  33.6 1.9 %collective-permute-start.5 = (bf16[640,256]{1,0:T(8,128)(2,1)S(1)}, bf16[640,256]{1,0:T(8,128)(2,1)S(1)}, u32[]{:S(2)}, u32[]{:S(2)}) collective-permute-start(bf16[640,256]{1,0:T(8,128)(2,1)S(1)} %hand_on.5.refs_0_.refs_2_), channel_id=1, source_target_pairs={{0,8},{8,0},{16,24},{24,16},{32,40},{40,32},{48,56},{56,48},{64,72... | collective-permute-start | bytes 983048 | tf_op jit(solution)/shard_map/ppermute | solution.py:391
  33.7 13.4 %collective-permute-start.3 = (bf16[640,256]{1,0:T(8,128)(2,1)S(1)}, bf16[640,256]{1,0:T(8,128)(2,1)S(1)}, u32[]{:S(2)}, u32[]{:S(2)}) collective-permute-start(bf16[640,256]{1,0:T(8,128)(2,1)S(1)} %hand_on.4), channel_id=1, source_target_pairs={{0,8},{8,0},{16,24},{24,16},{32,40},{40,32},{48,56},{56,48},{64,72... | collective-permute-start | bytes 983048 | tf_op jit(solution)/shard_map/ppermute | solution.py:389
  34.2 12.6 %collective-permute-start.8 = (bf16[640,256]{1,0:T(8,128)(2,1)S(1)}, bf16[640,256]{1,0:T(8,128)(2,1)S(1)}, u32[]{:S(2)}, u32[]{:S(2)}) collective-permute-start(bf16[640,256]{1,0:T(8,128)(2,1)S(1)} %hand_on.5.refs_0_.refs_2_), channel_id=1, source_target_pairs={{32,64},{40,72},{48,80},{56,88},{64,96},{72,104},{80,112},{88,120}... | collective-permute-start | bytes 983048 | tf_op jit(solution)/shard_map/ppermute | solution.py:390
  46.9 3.9 %collective-permute-start.9 = (bf16[640,256]{1,0:T(8,128)(2,1)S(1)}, bf16[640,256]{1,0:T(8,128)(2,1)S(1)}, u32[]{:S(2)}, u32[]{:S(2)}) collective-permute-start(bf16[640,256]{1,0:T(8,128)(2,1)S(1)} %hand_on.7.refs_6_), channel_id=1, source_target_pairs={{0,8},{8,0},{16,24},{24,16},{32,40},{40,32},{48,56},{56,48},{64,72... | collective-permute-start | bytes 983048 | tf_op jit(solution)/shard_map/ppermute | solution.py:395

commit v4 on v3

--- a/solution.py
+++ b/solution.py
@@ -41,59 +41,46 @@
     return slice(r * HD, (r + 1) * HD)
 
 
-def select_kernel(core_ref, rows_ref, kv_ref, side_ref, out_ref, half_ref):
-    rows = rows_ref[...]
+def select_kernel(rows_ref, kv_ref, out_ref):
     ids = lax.broadcasted_iota(jnp.int32, (BLK, PASS), 0)
-    picked = jnp.where(ids == rows, 1.0, 0.0).astype(BF16)
+    picked = jnp.where(ids == rows_ref[...], 1.0, 0.0).astype(BF16)
     out_ref[...] = lax.dot_general(
         picked, kv_ref[...], (((0,), (0,)), ((), ())), preferred_element_type=F32
     ).astype(BF16)
 
-    @pl.when(core_ref[0] == 0)
-    def _():
-        half_ref[...] = kv_ref[:HALF]
-
-    @pl.when(core_ref[0] != 0)
-    def _():
-        half_ref[...] = side_ref[HALF : 2 * HALF]
-
-
-def select(core, rows, kv, side):
+
+def select(rows, kv):
     return pl.pallas_call(
         select_kernel,
-        out_shape=(
-            jax.ShapeDtypeStruct((PASS, 2 * HD), BF16),
-            jax.ShapeDtypeStruct((HALF, 2 * HD), BF16),
-        ),
-        in_specs=[SMEM, VMEM, VMEM, VMEM],
-        out_specs=(VMEM, VMEM),
+        out_shape=jax.ShapeDtypeStruct((PASS, 2 * HD), BF16),
+        in_specs=[VMEM, VMEM],
+        out_specs=VMEM,
         compiler_params=params(),
         name="select_rows",
-    )(core, rows, kv, side)
-
-
-def join_kernel(where_ref, mine_ref, peer_ref, half_ref, peer_half_ref, out_ref):
+    )(rows, kv)
+
+
+def join_kernel(me_ref, mine_ref, peer_ref, kv_ref, *refs):
+    halves, out_ref = refs[:-1], refs[-1]
     out_ref[:PASS] = mine_ref[...]
     out_ref[PASS : 2 * PASS] = peer_ref[...]
-
-    @pl.when(where_ref[0] == 0)
-    def _():
-        out_ref[2 * PASS :] = half_ref[...]
-
-    @pl.when(where_ref[0] != 0)
-    def _():
-        out_ref[2 * PASS :] = peer_half_ref[...]
-
-
-def join(where, mine, peer, half, peer_half):
+    out_ref[2 * PASS :] = kv_ref[:HALF]
+    for block, half_ref in enumerate(halves):
+
+        @pl.when(me_ref[0] == block + 1)
+        def _():
+            out_ref[2 * PASS :] = half_ref[...]
+
+
+def join(me, mine, peer, kv, halves):
     return pl.pallas_call(
         join_kernel,
         out_shape=jax.ShapeDtypeStruct((2 * PASS + HALF, 2 * HD), BF16),
-        in_specs=[SMEM, VMEM, VMEM, VMEM, VMEM],
+        in_specs=[SMEM] + [VMEM] * (3 + len(halves)),
         out_specs=VMEM,
         compiler_params=params(),
         name="join_rows",
-    )(where, mine, peer, half, peer_half)
+    )(me, mine, peer, kv, *halves)
 
 
 def powers(scores):
@@ -351,11 +338,13 @@
     ).transpose(1, 0, 2)
     kv = lax.all_to_all(both, "head", split_axis=0, concat_axis=0, tiled=True).reshape(BLK, 2 * HD)
 
-    anchor_side = move(kv[: 2 * HALF], perm=[(0, 1)])
-    mine, half = select(flags(c), passing_rows, kv, anchor_side)
+    mine = select(passing_rows, kv)
     peer = move(mine, perm=PEER)
-    peer_half = move(half, perm=[(0, 2), (1, 3)])
-    pair = join(flags(h), mine, peer, half, peer_half)
+    low, high = kv[:HALF], kv[HALF : 2 * HALF]
+    halves = [
+        move(half, perm=[(0, block)]) for block, half in ((1, high), (2, low), (3, high))
+    ]
+    pair = join(flags(me), mine, peer, kv, halves)
     one = move(pair, perm=ahead(1))
     three = move(pair, perm=ahead(3))
 

time: 177 us -> 176 us (level)
  waiting for transfers between devices: 6.72 us -> 4.1 us
  transfers between devices with their start and end apart: 10 -> 11, of which waited for: 2 -> 2; matrix products, arithmetic and copies ran while one was open for 0% -> 0% of each run, Pallas kernels for 11% -> 11%
where the time goes in v4:
time: 176 us
  Pallas kernels  145 us (82%)
  starting transfers between devices  11.4 us (6%)
  blocking collectives  10.8 us (6%)
  waiting for transfers between devices  4.1 us (2%)
  local copies, waits for them, and re-layouts  3.91 us (2%)
    pallas_call x1, Pallas kernels, final(): pl.pallas_call(functools.partial(final_kernel, earlier, last, idle), out_...  126 us
    pallas_call x2, Pallas kernels, stage(): pl.pallas_call(functools.partial(stage_kernel, fresh, more, idle), out_sh...  15 us
    all_to_all x1, blocking collectives, local(): lax.all_to_all(both, 'head', split_axis=0, concat_axis=0, tiled=True)  10.8 us
    ppermute x1, starting transfers between devices, local(): arrays[4], arrays[5] = (three, move(three, perm=SIBLING))  4.25 us
    pallas_call x1, Pallas kernels, first_part(): pl.pallas_call(functools.partial(first_kernel, groups), out_shape=(jax.Sh...  3.84 us
  transfers between devices with their start and end apart: 11, of which 2 were waited for; matrix products, arithmetic and copies ran while one was open for 0% of the time, Pallas kernels for 11%

profile of v4, /device:TPU:113, one launch (start us, length us, event | category | flops | bytes accessed | tf_op | source)
XLA Modules:
  0.0 175.6 jit_solution(15355822959069557567)
XLA Ops:
  0.0 0.0 copy-start
  0.0 0.9 copy-done
  0.9 1.0 copy_bitcast_fusion
  1.9 10.8 %all_to_all.5 = bf16[8,64,256]{2,1,0:T(8,128)(2,1)S(1)} all-to-all(bf16[8,64,256]{2,1,0:T(8,128)(2,1)S(1)} %maximum_bitcast_fusion), channel_id=1, replica_groups=mesh['seq'=16,'head'=8] {'head'}, dimensions={0} | all-to-all | bytes 524288 | tf_op jit(solution)/shard_map/all_to_all | solution.py:339
  12.7 0.0 copy-start.1
  12.7 0.7 copy-done.1
  13.4 0.3 select_rows.1.mine_ref
  13.7 0.4 collective-permute-start
  14.1 0.7 collective-permute-start.1
  14.8 0.7 collective-permute-start.3
  15.5 0.7 collective-permute-start.2
  16.2 0.0 collective-permute-done.1.refs_0_
  16.2 0.0 collective-permute-done.3.refs_2_
  16.2 0.0 collective-permute-done.2.refs_1_
  16.2 2.9 %collective-permute-done.peer_ref = bf16[256,256]{1,0:T(8,128)(2,1)S(1)} collective-permute-done((bf16[256,256]{1,0:T(8,128)(2,1)S(1)}, bf16[256,256]{1,0:T(8,128)(2,1)S(1)}, u32[]{:S(2)}, u32[]{:S(2)}) %collective-permute-start) | collective-permute-done | bytes 131104 | tf_op jit(solution)/shard_map/ppermute | solution.py:342
  19.1 1.3 collective-permute-start.7
  20.4 1.3 collective-permute-start.5
  21.8 0.1 stack.68
  21.9 0.0 copy-start.2
  21.9 1.2 copy-done.2
  23.2 0.0 copy-start.3
  23.2 3.8 %first_blocks.1 = (f32[8,512,256]{2,1,0:T(8,128)S(1)}, f32[8,128]{1,0:T(8,128)S(1)}) custom-call(s32[12]{0:T(128)S(1)} %stack.69.use_ref, bf16[512,1024]{1,0:T(8,128)(2,1)S(1)} %copy-done.2, bf16[512,256]{1,0:T(8,128)(2,1)S(1)} %bitcast.30, bf16[640,256]{1,0:T(8,128)(2,1)S(1)} %join_rows.1.refs_0_), custom_call_target="tpu_custom_call" | custom-call | flops 2684354560 | bytes 1048576 | tf_op jit(solution)/shard_map/first_blocks/pallas_call | solution.py:121
  27.0 1.2 collective-permute-done.7.refs_0_
  28.2 4.2 %collective-permute-start.8 = (bf16[640,256]{1,0:T(8,128)(2,1)S(1)}, bf16[640,256]{1,0:T(8,128)(2,1)S(1)}, u32[]{:S(2)}, u32[]{:S(2)}) collective-permute-start(bf16[640,256]{1,0:T(8,128)(2,1)S(1)} %hand_on.6.refs_2_.refs_4_), channel_id=1, source_target_pairs={{0,8},{8,0},{16,24},{24,16},{32,40},{40,32},{48,56},{56,48},{64,72... | collective-permute-start | bytes 983048 | tf_op jit(solution)/shard_map/ppermute | solution.py:381
  32.4 0.0 collective-permute-done.5.refs_0_
  32.4 0.1 collective-permute-start.6
  32.5 0.5 collective-permute-start.4
  33.1 1.3 collective-permute-start.9
  34.3 0.0 collective-permute-done.8.refs_3_.refs_5_
  34.4 0.0 collective-permute-done.6.refs_1_.refs_3_
  34.4 0.0 copy-done.3
  34.4 11.3 %add_blocks.2 = (f32[8,512,256]{2,1,0:T(8,128)S(1)}, f32[8,128]{1,0:T(8,128)S(1)}) custom-call(s32[12]{0:T(128)S(1)} %stack.69.use_ref, bf16[512,1024]{1,0:T(8,128)(2,1)S(1)} %copy-done.3, bf16[640,256]{1,0:T(8,128)(2,1)S(1)} %hand_on.5.refs_0_.refs_2_, bf16[640,256]{1,0:T(8,128)(2,1)S(1)} %collective-permute-done.6.refs_1_.refs_3_, ...), custom_call_target="tpu_custom_call" | custom-call | flops 9663676416 | bytes 1048576 | tf_op jit(solution)/shard_map/add_blocks/pallas_call | solution.py:202
  45.7 0.0 collective-permute-done.9.refs_0_
  45.7 0.2 collective-permute-start.10
  45.9 0.0 collective-permute-done.4.refs_1_
  45.9 3.7 %add_blocks.3 = (f32[8,512,256]{2,1,0:T(8,128)S(1)}, f32[8,128]{1,0:T(8,128)}) custom-call(s32[12]{0:T(128)S(1)} %stack.69.use_ref, bf16[512,1024]{1,0:T(8,128)(2,1)S(1)} %copy-done.3, bf16[640,256]{1,0:T(8,128)(2,1)S(1)} %join_rows.1.refs_0_, bf16[640,256]{1,0:T(8,128)(2,1)S(1)} %collective-permute-done.4.refs_1_, f32[8,512,256]{2,1,0:T(8,128)S(1)} %get-tuple-element.13.refs_2_), custom_call_target="tpu_custom_call" | custom-call | flops 2147483648 | bytes 1048576 | tf_op jit(solution)/shard_map/add_blocks/pallas_call | solution.py:202
  49.6 0.0 collective-permute-done.10.refs_7_
  49.6 125.8 %last_blocks.1 = bf16[512,1024]{1,0:T(8,128)(2,1)} custom-call(s32[12]{0:T(128)S(1)} %stack.69.use_ref, bf16[512,1024]{1,0:T(8,128)(2,1)S(1)} %copy-done.3, bf16[640,256]{1,0:T(8,128)(2,1)S(1)} %join_rows.1.refs_0_, bf16[640,256]{1,0:T(8,128)(2,1)S(1)} %collective-permute-done.4.refs_1_, bf16[640,256]{1,0:T(8,128)(2,1)S(1)} %hand_on.5.refs_0_.refs_2_, ...), custom_call_target="tpu_custom_call" | custom-call | flops 4294967296 | bytes 1048576 | tf_op jit(solution)/shard_map/last_blocks/pallas_call | solution.py:285
  (9 shorter events, 0.1 us)
Async XLA Ops:
  0.0 0.9 copy-start
  12.7 0.7 copy-start.1
  13.7 5.4 %collective-permute-start = (bf16[256,256]{1,0:T(8,128)(2,1)S(1)}, bf16[256,256]{1,0:T(8,128)(2,1)S(1)}, u32[]{:S(2)}, u32[]{:S(2)}) collective-permute-start(bf16[256,256]{1,0:T(8,128)(2,1)S(1)} %select_rows.1.mine_ref), channel_id=1, source_target_pairs={{0,16},{8,24},{16,0},{24,8},{32,48},{40,56},{48,32},{56,40},{64,80... | collective-permute-start | bytes 393224 | tf_op jit(solution)/shard_map/ppermute | solution.py:342
  14.1 2.0 %collective-permute-start.1 = (bf16[128,256]{1,0:T(8,128)(2,1)S(1)}, bf16[128,256]{1,0:T(8,128)(2,1)S(1)}, u32[]{:S(2)}, u32[]{:S(2)}) collective-permute-start(bf16[128,256]{1,0:T(8,128)(2,1)S(1)} %bitcast.33), channel_id=1, source_target_pairs={{0,8},{1,9},{2,10},{3,11},{4,12},{5,13},{6,14},{7,15}} | collective-permute-start | bytes 196616 | tf_op jit(solution)/shard_map/ppermute | solution.py:345
  14.8 1.4 collective-permute-start.3
  15.5 0.7 collective-permute-start.2
  19.1 9.0 %collective-permute-start.7 = (bf16[640,256]{1,0:T(8,128)(2,1)S(1)}, bf16[640,256]{1,0:T(8,128)(2,1)S(1)}, u32[]{:S(2)}, u32[]{:S(2)}) collective-permute-start(bf16[640,256]{1,0:T(8,128)(2,1)S(1)} %join_rows.1.refs_0_), channel_id=1, source_target_pairs={{0,96},{8,104},{16,112},{24,120},{1,97},{9,105},{17,113},{25,121},... | collective-permute-start | bytes 983048 | tf_op jit(solution)/shard_map/ppermute | solution.py:349
  20.4 12.0 %collective-permute-start.5 = (bf16[640,256]{1,0:T(8,128)(2,1)S(1)}, bf16[640,256]{1,0:T(8,128)(2,1)S(1)}, u32[]{:S(2)}, u32[]{:S(2)}) collective-permute-start(bf16[640,256]{1,0:T(8,128)(2,1)S(1)} %join_rows.1.refs_0_), channel_id=1, source_target_pairs={{0,32},{8,40},{16,48},{24,56},{32,64},{40,72},{48,80},{56,88},{64,... | collective-permute-start | bytes 983048 | tf_op jit(solution)/shard_map/ppermute | solution.py:348
  21.9 1.2 copy-start.2
  23.2 11.2 %copy-start.3 = (bf16[512,1024]{1,0:T(8,128)(2,1)S(1)}, bf16[512,1024]{1,0:T(8,128)(2,1)}, u32[]{:S(2)}) copy-start(bf16[512,1024]{1,0:T(8,128)(2,1)} %q_ref.7) | copy-start | bytes 3145732
  28.2 6.2 %collective-permute-start.8 = (bf16[640,256]{1,0:T(8,128)(2,1)S(1)}, bf16[640,256]{1,0:T(8,128)(2,1)S(1)}, u32[]{:S(2)}, u32[]{:S(2)}) collective-permute-start(bf16[640,256]{1,0:T(8,128)(2,1)S(1)} %hand_on.6.refs_2_.refs_4_), channel_id=1, source_target_pairs={{0,8},{8,0},{16,24},{24,16},{32,40},{40,32},{48,56},{56,48},{64,72... | collective-permute-start | bytes 983048 | tf_op jit(solution)/shard_map/ppermute | solution.py:381
  32.4 1.9 %collective-permute-start.6 = (bf16[640,256]{1,0:T(8,128)(2,1)S(1)}, bf16[640,256]{1,0:T(8,128)(2,1)S(1)}, u32[]{:S(2)}, u32[]{:S(2)}) collective-permute-start(bf16[640,256]{1,0:T(8,128)(2,1)S(1)} %hand_on.5.refs_0_.refs_2_), channel_id=1, source_target_pairs={{0,8},{8,0},{16,24},{24,16},{32,40},{40,32},{48,56},{56,48},{64,72... | collective-permute-start | bytes 983048 | tf_op jit(solution)/shard_map/ppermute | solution.py:380
  32.5 13.4 %collective-permute-start.4 = (bf16[640,256]{1,0:T(8,128)(2,1)S(1)}, bf16[640,256]{1,0:T(8,128)(2,1)S(1)}, u32[]{:S(2)}, u32[]{:S(2)}) collective-permute-start(bf16[640,256]{1,0:T(8,128)(2,1)S(1)} %hand_on.4), channel_id=1, source_target_pairs={{0,8},{8,0},{16,24},{24,16},{32,40},{40,32},{48,56},{56,48},{64,72... | collective-permute-start | bytes 983048 | tf_op jit(solution)/shard_map/ppermute | solution.py:378
  33.1 12.6 %collective-permute-start.9 = (bf16[640,256]{1,0:T(8,128)(2,1)S(1)}, bf16[640,256]{1,0:T(8,128)(2,1)S(1)}, u32[]{:S(2)}, u32[]{:S(2)}) collective-permute-start(bf16[640,256]{1,0:T(8,128)(2,1)S(1)} %hand_on.5.refs_0_.refs_2_), channel_id=1, source_target_pairs={{32,64},{40,72},{48,80},{56,88},{64,96},{72,104},{80,112},{88,120}... | collective-permute-start | bytes 983048 | tf_op jit(solution)/shard_map/ppermute | solution.py:379
  45.7 3.9 %collective-permute-start.10 = (bf16[640,256]{1,0:T(8,128)(2,1)S(1)}, bf16[640,256]{1,0:T(8,128)(2,1)S(1)}, u32[]{:S(2)}, u32[]{:S(2)}) collective-permute-start(bf16[640,256]{1,0:T(8,128)(2,1)S(1)} %hand_on.7.refs_6_), channel_id=1, source_target_pairs={{0,8},{8,0},{16,24},{24,16},{32,40},{40,32},{48,56},{56,48},{64,72... | collective-permute-start | bytes 983048 | tf_op jit(solution)/shard_map/ppermute | solution.py:384

commit v5 on v4

--- a/solution.py
+++ b/solution.py
@@ -12,7 +12,7 @@
 BLK = 512
 PASS = 256
 HALF = 128
-SIDE = 4
+SIDE = 8
 SCALE = float(HD**-0.5 * 1.4426950408889634)
 LOW, HIGH = 2.0**-80, 2.0**100
 BF16, F32 = jnp.bfloat16, jnp.float32
@@ -41,23 +41,46 @@
     return slice(r * HD, (r + 1) * HD)
 
 
-def select_kernel(rows_ref, kv_ref, out_ref):
+def mark_kernel(rows_ref, picked_ref):
     ids = lax.broadcasted_iota(jnp.int32, (BLK, PASS), 0)
-    picked = jnp.where(ids == rows_ref[...], 1.0, 0.0).astype(BF16)
+    picked_ref[...] = jnp.where(ids == rows_ref[...], 1.0, 0.0).astype(BF16)
+
+
+def mark(rows):
+    return pl.pallas_call(
+        mark_kernel,
+        out_shape=jax.ShapeDtypeStruct((BLK, PASS), BF16),
+        in_specs=[VMEM],
+        out_specs=VMEM,
+        compiler_params=params(),
+        cost_estimate=cost(1),
+        name="mark_rows",
+    )(rows)
+
+
+def select_kernel(picked_ref, parts_ref, out_ref, kv_ref):
+    count = parts_ref.shape[2]
+    for part in range(GROUP):
+        rows = slice(part * count, (part + 1) * count)
+        kv_ref[rows, :HD] = parts_ref[part, 0]
+        kv_ref[rows, HD:] = parts_ref[part, 1]
     out_ref[...] = lax.dot_general(
-        picked, kv_ref[...], (((0,), (0,)), ((), ())), preferred_element_type=F32
+        picked_ref[...], kv_ref[...], (((0,), (0,)), ((), ())), preferred_element_type=F32
     ).astype(BF16)
 
 
-def select(rows, kv):
+def select(picked, parts):
     return pl.pallas_call(
         select_kernel,
-        out_shape=jax.ShapeDtypeStruct((PASS, 2 * HD), BF16),
+        out_shape=(
+            jax.ShapeDtypeStruct((PASS, 2 * HD), BF16),
+            jax.ShapeDtypeStruct((BLK, 2 * HD), BF16),
+        ),
         in_specs=[VMEM, VMEM],
-        out_specs=VMEM,
+        out_specs=(VMEM, VMEM),
         compiler_params=params(),
         name="select_rows",
-    )(rows, kv)
+    )(picked, parts)
 
 
 def join_kernel(me_ref, mine_ref, peer_ref, kv_ref, *refs):
@@ -333,12 +356,13 @@
 
     kv_heads = key_states.shape[1] // HD
     rows = key_states.shape[0]
-    both = jnp.concatenate(
-        [key_states.reshape(rows, kv_heads, HD), value_states.reshape(rows, kv_heads, HD)], axis=2
-    ).transpose(1, 0, 2)
-    kv = lax.all_to_all(both, "head", split_axis=0, concat_axis=0, tiled=True).reshape(BLK, 2 * HD)
-
-    mine = select(passing_rows, kv)
+    by_head = [
+        x.reshape(rows, kv_heads, HD).transpose(1, 0, 2) for x in (key_states, value_states)
+    ]
+    parts = lax.all_to_all(
+        jnp.stack(by_head, axis=1), "head", split_axis=0, concat_axis=0, tiled=True
+    )
+    mine, kv = select(mark(passing_rows), parts)
     peer = move(mine, perm=PEER)
     low, high = kv[:HALF], kv[HALF : 2 * HALF]
     halves = [

time: 176 us -> 176 us (level)
  blocking collectives: 10.8 us -> 0 us
  waiting for transfers between devices: 4.1 us -> 10.9 us
  starting transfers between devices: 11.4 us -> 16.1 us
    all_to_all x1 -> x0, blocking collectives: 10.8 us -> none  [local(): lax.all_to_all(both, 'head', split_axis=0, concat_axis=0, tiled=True)]
    all_to_all x0 -> x1, waiting for transfers between devices: none -> 5.56 us  [local(): lax.all_to_all(jnp.stack(by_head, axis=1), 'head', split_axis=0, concat_a...]
    all_to_all x0 -> x1, starting transfers between devices: none -> 4.74 us  [local(): lax.all_to_all(jnp.stack(by_head, axis=1), 'head', split_axis=0, concat_a...]
  transfers between devices with their start and end apart: 11 -> 12, of which waited for: 2 -> 3; matrix products, arithmetic and copies ran while one was open for 0% -> 0% of each run, Pallas kernels for 11% -> 11%
where the time goes in v5:
time: 176 us
  Pallas kernels  145 us (82%)
  starting transfers between devices  16.1 us (9%)
  waiting for transfers between devices  10.9 us (6%)
  local copies, waits for them, and re-layouts  2.77 us (2%)
    pallas_call x1, Pallas kernels, final(): pl.pallas_call(functools.partial(final_kernel, earlier, last, idle), out_...  126 us
    pallas_call x2, Pallas kernels, stage(): pl.pallas_call(functools.partial(stage_kernel, fresh, more, idle), out_sh...  15 us
    all_to_all x1, waiting for transfers between devices, local(): lax.all_to_all(jnp.stack(by_head, axis=1), 'head', split_axis=0, concat_a...  5.56 us
    all_to_all x1, starting transfers between devices, local(): lax.all_to_all(jnp.stack(by_head, axis=1), 'head', split_axis=0, concat_a...  4.74 us
    ppermute x1, starting transfers between devices, local(): arrays[4], arrays[5] = (three, move(three, perm=SIBLING))  4.25 us
    pallas_call x1, Pallas kernels, first_part(): pl.pallas_call(functools.partial(first_kernel, groups), out_shape=(jax.Sh...  3.85 us
  transfers between devices with their start and end apart: 12, of which 3 were waited for; matrix products, arithmetic and copies ran while one was open for 0% of the time, Pallas kernels for 11%

profile of v5, /device:TPU:113, one launch (start us, length us, event | category | flops | bytes accessed | tf_op | source)
XLA Modules:
  0.0 175.9 jit_solution(6456715431783471431)
XLA Ops:
  0.0 0.0 copy-start
  0.0 0.9 copy-done
  0.9 0.0 copy-start.1
  0.9 1.0 bitcast_bitcast_fusion
  2.0 0.7 pad_maximum_fusion
  2.7 4.7 %all-to-all-start = ((bf16[8,2,64,128]{3,2,1,0:T(8,128)(2,1)}), bf16[8,2,64,128]{3,2,1,0:T(8,128)(2,1)S(1)}, u32[]{:S(2)}, u32[]{:S(2)}) async-start(bf16[8,2,64,128]{3,2,1,0:T(8,128)(2,1)} %pad_maximum_fusion), calls=%async_computation | async-start | bytes 524288 | tf_op jit(solution)/shard_map/all_to_all | solution.py:362
  7.4 0.0 copy-start.2
  7.4 0.7 copy-done.2
  8.1 0.1 mark_rows.1.picked_ref
  8.2 5.6 %all-to-all-done.parts_ref = bf16[8,2,64,128]{3,2,1,0:T(8,128)(2,1)S(1)} async-done(((bf16[8,2,64,128]{3,2,1,0:T(8,128)(2,1)}), bf16[8,2,64,128]{3,2,1,0:T(8,128)(2,1)S(1)}, u32[]{:S(2)}, u32[]{:S(2)}) %all-to-all-start) | async-done | bytes 262176 | tf_op jit(solution)/shard_map/all_to_all | solution.py:362
  13.7 0.3 select_rows.1
  14.0 0.4 collective-permute-start
  14.5 0.7 collective-permute-start.1
  15.1 0.7 collective-permute-start.3
  15.8 0.7 collective-permute-start.2
  16.5 0.0 collective-permute-done.1.refs_0_
  16.5 0.0 collective-permute-done.3.refs_2_
  16.5 0.0 collective-permute-done.2.refs_1_
  16.5 2.9 %collective-permute-done.peer_ref = bf16[256,256]{1,0:T(8,128)(2,1)S(1)} collective-permute-done((bf16[256,256]{1,0:T(8,128)(2,1)S(1)}, bf16[256,256]{1,0:T(8,128)(2,1)S(1)}, u32[]{:S(2)}, u32[]{:S(2)}) %collective-permute-start) | collective-permute-done | bytes 131104 | tf_op jit(solution)/shard_map/ppermute | solution.py:366
  19.5 1.3 collective-permute-start.7
  20.8 1.3 collective-permute-start.5
  22.1 0.1 stack.77
  22.2 0.0 copy-done.1
  22.3 3.9 %first_blocks.1 = (f32[8,512,256]{2,1,0:T(8,128)S(1)}, f32[8,128]{1,0:T(8,128)S(1)}) custom-call(s32[12]{0:T(128)S(1)} %stack.78.use_ref, bf16[512,1024]{1,0:T(8,128)(2,1)S(1)} %copy-done.1, bf16[512,256]{1,0:T(8,128)(2,1)S(1)} %get-tuple-element.13.kv_ref.refs_8_, bf16[640,256]{1,0:T(8,128)(2,1)S(1)} %join_rows.1.refs_0_), custom_call_target="tpu_custom_call" | custom-call | flops 2684354560 | bytes 1048576 | tf_op jit(solution)/shard_map/first_blocks/pallas_call | solution.py:144
  26.1 2.4 %collective-permute-done.7.refs_0_ = bf16[640,256]{1,0:T(8,128)(2,1)S(1)} collective-permute-done((bf16[640,256]{1,0:T(8,128)(2,1)S(1)}, bf16[640,256]{1,0:T(8,128)(2,1)S(1)}, u32[]{:S(2)}, u32[]{:S(2)}) %collective-permute-start.7) | collective-permute-done | bytes 327712 | tf_op jit(solution)/shard_map/ppermute | solution.py:373
  28.5 4.2 %collective-permute-start.8 = (bf16[640,256]{1,0:T(8,128)(2,1)S(1)}, bf16[640,256]{1,0:T(8,128)(2,1)S(1)}, u32[]{:S(2)}, u32[]{:S(2)}) collective-permute-start(bf16[640,256]{1,0:T(8,128)(2,1)S(1)} %hand_on.6.refs_2_.refs_4_), channel_id=1, source_target_pairs={{0,8},{8,0},{16,24},{24,16},{32,40},{40,32},{48,56},{56,48},{64,72... | collective-permute-start | bytes 983048 | tf_op jit(solution)/shard_map/ppermute | solution.py:405
  32.7 0.0 collective-permute-done.5.refs_0_
  32.7 0.1 collective-permute-start.6
  32.9 0.5 collective-permute-start.4
  33.4 1.3 collective-permute-start.9
  34.7 0.0 collective-permute-done.8.refs_3_.refs_5_
  34.7 0.0 collective-permute-done.6.refs_1_.refs_3_
  34.7 11.3 %add_blocks.2 = (f32[8,512,256]{2,1,0:T(8,128)S(1)}, f32[8,128]{1,0:T(8,128)S(1)}) custom-call(s32[12]{0:T(128)S(1)} %stack.78.use_ref, bf16[512,1024]{1,0:T(8,128)(2,1)S(1)} %copy-done.1, bf16[640,256]{1,0:T(8,128)(2,1)S(1)} %hand_on.5.refs_0_.refs_2_, bf16[640,256]{1,0:T(8,128)(2,1)S(1)} %collective-permute-done.6.refs_1_.refs_3_, ...), custom_call_target="tpu_custom_call" | custom-call | flops 9663676416 | bytes 1048576 | tf_op jit(solution)/shard_map/add_blocks/pallas_call | solution.py:225
  46.0 0.0 collective-permute-done.9.refs_0_
  46.0 0.2 collective-permute-start.10
  46.2 0.0 collective-permute-done.4.refs_1_
  46.2 3.7 %add_blocks.3 = (f32[8,512,256]{2,1,0:T(8,128)S(1)}, f32[8,128]{1,0:T(8,128)}) custom-call(s32[12]{0:T(128)S(1)} %stack.78.use_ref, bf16[512,1024]{1,0:T(8,128)(2,1)S(1)} %copy-done.1, bf16[640,256]{1,0:T(8,128)(2,1)S(1)} %join_rows.1.refs_0_, bf16[640,256]{1,0:T(8,128)(2,1)S(1)} %collective-permute-done.4.refs_1_, f32[8,512,256]{2,1,0:T(8,128)S(1)} %get-tuple-element.17.refs_2_), custom_call_target="tpu_custom_call" | custom-call | flops 2147483648 | bytes 1048576 | tf_op jit(solution)/shard_map/add_blocks/pallas_call | solution.py:225
  49.9 0.0 collective-permute-done.10.refs_7_
  49.9 125.8 %last_blocks.1 = bf16[512,1024]{1,0:T(8,128)(2,1)} custom-call(s32[12]{0:T(128)S(1)} %stack.78.use_ref, bf16[512,1024]{1,0:T(8,128)(2,1)S(1)} %copy-done.1, bf16[640,256]{1,0:T(8,128)(2,1)S(1)} %join_rows.1.refs_0_, bf16[640,256]{1,0:T(8,128)(2,1)S(1)} %collective-permute-done.4.refs_1_, bf16[640,256]{1,0:T(8,128)(2,1)S(1)} %hand_on.5.refs_0_.refs_2_, ...), custom_call_target="tpu_custom_call" | custom-call | flops 4294967296 | bytes 1048576 | tf_op jit(solution)/shard_map/last_blocks/pallas_call | solution.py:308
  (8 shorter events, 0.1 us)
Async XLA Ops:
  0.0 0.9 copy-start
  0.9 21.3 %copy-start.1 = (bf16[512,1024]{1,0:T(8,128)(2,1)S(1)}, bf16[512,1024]{1,0:T(8,128)(2,1)}, u32[]{:S(2)}) copy-start(bf16[512,1024]{1,0:T(8,128)(2,1)} %q_ref.7) | copy-start | bytes 3145732
  2.7 11.0 %all-to-all-start = ((bf16[8,2,64,128]{3,2,1,0:T(8,128)(2,1)}), bf16[8,2,64,128]{3,2,1,0:T(8,128)(2,1)S(1)}, u32[]{:S(2)}, u32[]{:S(2)}) async-start(bf16[8,2,64,128]{3,2,1,0:T(8,128)(2,1)} %pad_maximum_fusion), calls=%async_computation | async-start | bytes 524288 | tf_op jit(solution)/shard_map/all_to_all | solution.py:362
  7.4 0.7 copy-start.2
  14.0 5.4 %collective-permute-start = (bf16[256,256]{1,0:T(8,128)(2,1)S(1)}, bf16[256,256]{1,0:T(8,128)(2,1)S(1)}, u32[]{:S(2)}, u32[]{:S(2)}) collective-permute-start(bf16[256,256]{1,0:T(8,128)(2,1)S(1)} %get-tuple-element.12.mine_ref), channel_id=1, source_target_pairs={{0,16},{8,24},{16,0},{24,8},{32,48},{40,56},{48,32},{56,40},{64,80... | collective-permute-start | bytes 393224 | tf_op jit(solution)/shard_map/ppermute | solution.py:366
  14.5 2.0 %collective-permute-start.1 = (bf16[128,256]{1,0:T(8,128)(2,1)S(1)}, bf16[128,256]{1,0:T(8,128)(2,1)S(1)}, u32[]{:S(2)}, u32[]{:S(2)}) collective-permute-start(bf16[128,256]{1,0:T(8,128)(2,1)S(1)} %get-tuple-element.20), channel_id=1, source_target_pairs={{0,8},{1,9},{2,10},{3,11},{4,12},{5,13},{6,14},{7,15}} | collective-permute-start | bytes 196616 | tf_op jit(solution)/shard_map/ppermute | solution.py:369
  15.1 1.4 collective-permute-start.3
  15.8 0.7 collective-permute-start.2
  19.5 9.0 %collective-permute-start.7 = (bf16[640,256]{1,0:T(8,128)(2,1)S(1)}, bf16[640,256]{1,0:T(8,128)(2,1)S(1)}, u32[]{:S(2)}, u32[]{:S(2)}) collective-permute-start(bf16[640,256]{1,0:T(8,128)(2,1)S(1)} %join_rows.1.refs_0_), channel_id=1, source_target_pairs={{0,96},{8,104},{16,112},{24,120},{1,97},{9,105},{17,113},{25,121},... | collective-permute-start | bytes 983048 | tf_op jit(solution)/shard_map/ppermute | solution.py:373
  20.8 12.0 %collective-permute-start.5 = (bf16[640,256]{1,0:T(8,128)(2,1)S(1)}, bf16[640,256]{1,0:T(8,128)(2,1)S(1)}, u32[]{:S(2)}, u32[]{:S(2)}) collective-permute-start(bf16[640,256]{1,0:T(8,128)(2,1)S(1)} %join_rows.1.refs_0_), channel_id=1, source_target_pairs={{0,32},{8,40},{16,48},{24,56},{32,64},{40,72},{48,80},{56,88},{64,... | collective-permute-start | bytes 983048 | tf_op jit(solution)/shard_map/ppermute | solution.py:372
  28.5 6.2 %collective-permute-start.8 = (bf16[640,256]{1,0:T(8,128)(2,1)S(1)}, bf16[640,256]{1,0:T(8,128)(2,1)S(1)}, u32[]{:S(2)}, u32[]{:S(2)}) collective-permute-start(bf16[640,256]{1,0:T(8,128)(2,1)S(1)} %hand_on.6.refs_2_.refs_4_), channel_id=1, source_target_pairs={{0,8},{8,0},{16,24},{24,16},{32,40},{40,32},{48,56},{56,48},{64,72... | collective-permute-start | bytes 983048 | tf_op jit(solution)/shard_map/ppermute | solution.py:405
  32.7 1.9 %collective-permute-start.6 = (bf16[640,256]{1,0:T(8,128)(2,1)S(1)}, bf16[640,256]{1,0:T(8,128)(2,1)S(1)}, u32[]{:S(2)}, u32[]{:S(2)}) collective-permute-start(bf16[640,256]{1,0:T(8,128)(2,1)S(1)} %hand_on.5.refs_0_.refs_2_), channel_id=1, source_target_pairs={{0,8},{8,0},{16,24},{24,16},{32,40},{40,32},{48,56},{56,48},{64,72... | collective-permute-start | bytes 983048 | tf_op jit(solution)/shard_map/ppermute | solution.py:404
  32.9 13.4 %collective-permute-start.4 = (bf16[640,256]{1,0:T(8,128)(2,1)S(1)}, bf16[640,256]{1,0:T(8,128)(2,1)S(1)}, u32[]{:S(2)}, u32[]{:S(2)}) collective-permute-start(bf16[640,256]{1,0:T(8,128)(2,1)S(1)} %hand_on.4), channel_id=1, source_target_pairs={{0,8},{8,0},{16,24},{24,16},{32,40},{40,32},{48,56},{56,48},{64,72... | collective-permute-start | bytes 983048 | tf_op jit(solution)/shard_map/ppermute | solution.py:402
  33.4 12.6 %collective-permute-start.9 = (bf16[640,256]{1,0:T(8,128)(2,1)S(1)}, bf16[640,256]{1,0:T(8,128)(2,1)S(1)}, u32[]{:S(2)}, u32[]{:S(2)}) collective-permute-start(bf16[640,256]{1,0:T(8,128)(2,1)S(1)} %hand_on.5.refs_0_.refs_2_), channel_id=1, source_target_pairs={{32,64},{40,72},{48,80},{56,88},{64,96},{72,104},{80,112},{88,120}... | collective-permute-start | bytes 983048 | tf_op jit(solution)/shard_map/ppermute | solution.py:403
  46.0 3.9 %collective-permute-start.10 = (bf16[640,256]{1,0:T(8,128)(2,1)S(1)}, bf16[640,256]{1,0:T(8,128)(2,1)S(1)}, u32[]{:S(2)}, u32[]{:S(2)}) collective-permute-start(bf16[640,256]{1,0:T(8,128)(2,1)S(1)} %hand_on.7.refs_6_), channel_id=1, source_target_pairs={{0,8},{8,0},{16,24},{24,16},{32,40},{40,32},{48,56},{56,48},{64,72... | collective-permute-start | bytes 983048 | tf_op jit(solution)/shard_map/ppermute | solution.py:408

commit v6 on v4

--- a/solution.py
+++ b/solution.py
@@ -12,7 +12,7 @@
 BLK = 512
 PASS = 256
 HALF = 128
-SIDE = 4
+SIDE = 8
 SCALE = float(HD**-0.5 * 1.4426950408889634)
 LOW, HIGH = 2.0**-80, 2.0**100
 BF16, F32 = jnp.bfloat16, jnp.float32

time: 176 us -> 176 us (level)
  no operation moved by 1% of the time
where the time goes in v6:
time: 176 us
  Pallas kernels  145 us (82%)
  starting transfers between devices  11.4 us (6%)
  blocking collectives  10.8 us (6%)
  waiting for transfers between devices  4.1 us (2%)
  local copies, waits for them, and re-layouts  3.91 us (2%)
    pallas_call x1, Pallas kernels, final(): pl.pallas_call(functools.partial(final_kernel, earlier, last, idle), out_...  126 us
    pallas_call x2, Pallas kernels, stage(): pl.pallas_call(functools.partial(stage_kernel, fresh, more, idle), out_sh...  15 us
    all_to_all x1, blocking collectives, local(): lax.all_to_all(both, 'head', split_axis=0, concat_axis=0, tiled=True)  10.8 us
    ppermute x1, starting transfers between devices, local(): arrays[4], arrays[5] = (three, move(three, perm=SIBLING))  4.25 us
    pallas_call x1, Pallas kernels, first_part(): pl.pallas_call(functools.partial(first_kernel, groups), out_shape=(jax.Sh...  3.84 us
  transfers between devices with their start and end apart: 11, of which 2 were waited for; matrix products, arithmetic and copies ran while one was open for 0% of the time, Pallas kernels for 11%

profile of v6, /device:TPU:113, one launch (start us, length us, event | category | flops | bytes accessed | tf_op | source)
XLA Modules:
  0.0 175.6 jit_solution(7142325340730132526)
XLA Ops:
  0.0 0.0 copy-start
  0.0 0.9 copy-done
  0.9 1.0 copy_bitcast_fusion
  1.9 10.8 %all_to_all.5 = bf16[8,64,256]{2,1,0:T(8,128)(2,1)S(1)} all-to-all(bf16[8,64,256]{2,1,0:T(8,128)(2,1)S(1)} %maximum_bitcast_fusion), channel_id=1, replica_groups=mesh['seq'=16,'head'=8] {'head'}, dimensions={0} | all-to-all | bytes 524288 | tf_op jit(solution)/shard_map/all_to_all | solution.py:339
  12.7 0.0 copy-start.1
  12.7 0.7 copy-done.1
  13.4 0.3 select_rows.1.mine_ref
  13.7 0.4 collective-permute-start
  14.1 0.7 collective-permute-start.1
  14.8 0.7 collective-permute-start.3
  15.5 0.7 collective-permute-start.2
  16.2 0.0 collective-permute-done.1.refs_0_
  16.2 0.0 collective-permute-done.3.refs_2_
  16.2 0.0 collective-permute-done.2.refs_1_
  16.2 2.9 %collective-permute-done.peer_ref = bf16[256,256]{1,0:T(8,128)(2,1)S(1)} collective-permute-done((bf16[256,256]{1,0:T(8,128)(2,1)S(1)}, bf16[256,256]{1,0:T(8,128)(2,1)S(1)}, u32[]{:S(2)}, u32[]{:S(2)}) %collective-permute-start) | collective-permute-done | bytes 131104 | tf_op jit(solution)/shard_map/ppermute | solution.py:342
  19.1 1.3 collective-permute-start.7
  20.4 1.3 collective-permute-start.5
  21.8 0.1 stack.68
  21.9 0.0 copy-start.2
  21.9 1.2 copy-done.2
  23.2 0.0 copy-start.3
  23.2 3.8 %first_blocks.1 = (f32[8,512,256]{2,1,0:T(8,128)S(1)}, f32[8,128]{1,0:T(8,128)S(1)}) custom-call(s32[12]{0:T(128)S(1)} %stack.69.use_ref, bf16[512,1024]{1,0:T(8,128)(2,1)S(1)} %copy-done.2, bf16[512,256]{1,0:T(8,128)(2,1)S(1)} %bitcast.30, bf16[640,256]{1,0:T(8,128)(2,1)S(1)} %join_rows.1.refs_0_), custom_call_target="tpu_custom_call" | custom-call | flops 2684354560 | bytes 1048576 | tf_op jit(solution)/shard_map/first_blocks/pallas_call | solution.py:121
  27.0 1.2 collective-permute-done.7.refs_0_
  28.2 4.2 %collective-permute-start.8 = (bf16[640,256]{1,0:T(8,128)(2,1)S(1)}, bf16[640,256]{1,0:T(8,128)(2,1)S(1)}, u32[]{:S(2)}, u32[]{:S(2)}) collective-permute-start(bf16[640,256]{1,0:T(8,128)(2,1)S(1)} %hand_on.6.refs_2_.refs_4_), channel_id=1, source_target_pairs={{0,8},{8,0},{16,24},{24,16},{32,40},{40,32},{48,56},{56,48},{64,72... | collective-permute-start | bytes 983048 | tf_op jit(solution)/shard_map/ppermute | solution.py:381
  32.4 0.0 collective-permute-done.5.refs_0_
  32.4 0.1 collective-permute-start.6
  32.5 0.5 collective-permute-start.4
  33.1 1.3 collective-permute-start.9
  34.3 0.0 collective-permute-done.8.refs_3_.refs_5_
  34.4 0.0 collective-permute-done.6.refs_1_.refs_3_
  34.4 0.0 copy-done.3
  34.4 11.3 %add_blocks.2 = (f32[8,512,256]{2,1,0:T(8,128)S(1)}, f32[8,128]{1,0:T(8,128)S(1)}) custom-call(s32[12]{0:T(128)S(1)} %stack.69.use_ref, bf16[512,1024]{1,0:T(8,128)(2,1)S(1)} %copy-done.3, bf16[640,256]{1,0:T(8,128)(2,1)S(1)} %hand_on.5.refs_0_.refs_2_, bf16[640,256]{1,0:T(8,128)(2,1)S(1)} %collective-permute-done.6.refs_1_.refs_3_, ...), custom_call_target="tpu_custom_call" | custom-call | flops 9663676416 | bytes 1048576 | tf_op jit(solution)/shard_map/add_blocks/pallas_call | solution.py:202
  45.7 0.0 collective-permute-done.9.refs_0_
  45.7 0.2 collective-permute-start.10
  45.9 0.0 collective-permute-done.4.refs_1_
  45.9 3.7 %add_blocks.3 = (f32[8,512,256]{2,1,0:T(8,128)S(1)}, f32[8,128]{1,0:T(8,128)}) custom-call(s32[12]{0:T(128)S(1)} %stack.69.use_ref, bf16[512,1024]{1,0:T(8,128)(2,1)S(1)} %copy-done.3, bf16[640,256]{1,0:T(8,128)(2,1)S(1)} %join_rows.1.refs_0_, bf16[640,256]{1,0:T(8,128)(2,1)S(1)} %collective-permute-done.4.refs_1_, f32[8,512,256]{2,1,0:T(8,128)S(1)} %get-tuple-element.13.refs_2_), custom_call_target="tpu_custom_call" | custom-call | flops 2147483648 | bytes 1048576 | tf_op jit(solution)/shard_map/add_blocks/pallas_call | solution.py:202
  49.6 0.0 collective-permute-done.10.refs_7_
  49.6 125.8 %last_blocks.1 = bf16[512,1024]{1,0:T(8,128)(2,1)} custom-call(s32[12]{0:T(128)S(1)} %stack.69.use_ref, bf16[512,1024]{1,0:T(8,128)(2,1)S(1)} %copy-done.3, bf16[640,256]{1,0:T(8,128)(2,1)S(1)} %join_rows.1.refs_0_, bf16[640,256]{1,0:T(8,128)(2,1)S(1)} %collective-permute-done.4.refs_1_, bf16[640,256]{1,0:T(8,128)(2,1)S(1)} %hand_on.5.refs_0_.refs_2_, ...), custom_call_target="tpu_custom_call" | custom-call | flops 4294967296 | bytes 1048576 | tf_op jit(solution)/shard_map/last_blocks/pallas_call | solution.py:285
  (9 shorter events, 0.1 us)
Async XLA Ops:
  0.0 0.9 copy-start
  12.7 0.7 copy-start.1
  13.7 5.4 %collective-permute-start = (bf16[256,256]{1,0:T(8,128)(2,1)S(1)}, bf16[256,256]{1,0:T(8,128)(2,1)S(1)}, u32[]{:S(2)}, u32[]{:S(2)}) collective-permute-start(bf16[256,256]{1,0:T(8,128)(2,1)S(1)} %select_rows.1.mine_ref), channel_id=1, source_target_pairs={{0,16},{8,24},{16,0},{24,8},{32,48},{40,56},{48,32},{56,40},{64,80... | collective-permute-start | bytes 393224 | tf_op jit(solution)/shard_map/ppermute | solution.py:342
  14.1 2.0 %collective-permute-start.1 = (bf16[128,256]{1,0:T(8,128)(2,1)S(1)}, bf16[128,256]{1,0:T(8,128)(2,1)S(1)}, u32[]{:S(2)}, u32[]{:S(2)}) collective-permute-start(bf16[128,256]{1,0:T(8,128)(2,1)S(1)} %bitcast.33), channel_id=1, source_target_pairs={{0,8},{1,9},{2,10},{3,11},{4,12},{5,13},{6,14},{7,15}} | collective-permute-start | bytes 196616 | tf_op jit(solution)/shard_map/ppermute | solution.py:345
  14.8 1.4 collective-permute-start.3
  15.5 0.7 collective-permute-start.2
  19.1 9.0 %collective-permute-start.7 = (bf16[640,256]{1,0:T(8,128)(2,1)S(1)}, bf16[640,256]{1,0:T(8,128)(2,1)S(1)}, u32[]{:S(2)}, u32[]{:S(2)}) collective-permute-start(bf16[640,256]{1,0:T(8,128)(2,1)S(1)} %join_rows.1.refs_0_), channel_id=1, source_target_pairs={{0,96},{8,104},{16,112},{24,120},{1,97},{9,105},{17,113},{25,121},... | collective-permute-start | bytes 983048 | tf_op jit(solution)/shard_map/ppermute | solution.py:349
  20.4 12.0 %collective-permute-start.5 = (bf16[640,256]{1,0:T(8,128)(2,1)S(1)}, bf16[640,256]{1,0:T(8,128)(2,1)S(1)}, u32[]{:S(2)}, u32[]{:S(2)}) collective-permute-start(bf16[640,256]{1,0:T(8,128)(2,1)S(1)} %join_rows.1.refs_0_), channel_id=1, source_target_pairs={{0,32},{8,40},{16,48},{24,56},{32,64},{40,72},{48,80},{56,88},{64,... | collective-permute-start | bytes 983048 | tf_op jit(solution)/shard_map/ppermute | solution.py:348
  21.9 1.2 copy-start.2
  23.2 11.2 %copy-start.3 = (bf16[512,1024]{1,0:T(8,128)(2,1)S(1)}, bf16[512,1024]{1,0:T(8,128)(2,1)}, u32[]{:S(2)}) copy-start(bf16[512,1024]{1,0:T(8,128)(2,1)} %q_ref.7) | copy-start | bytes 3145732
  28.2 6.2 %collective-permute-start.8 = (bf16[640,256]{1,0:T(8,128)(2,1)S(1)}, bf16[640,256]{1,0:T(8,128)(2,1)S(1)}, u32[]{:S(2)}, u32[]{:S(2)}) collective-permute-start(bf16[640,256]{1,0:T(8,128)(2,1)S(1)} %hand_on.6.refs_2_.refs_4_), channel_id=1, source_target_pairs={{0,8},{8,0},{16,24},{24,16},{32,40},{40,32},{48,56},{56,48},{64,72... | collective-permute-start | bytes 983048 | tf_op jit(solution)/shard_map/ppermute | solution.py:381
  32.4 1.9 %collective-permute-start.6 = (bf16[640,256]{1,0:T(8,128)(2,1)S(1)}, bf16[640,256]{1,0:T(8,128)(2,1)S(1)}, u32[]{:S(2)}, u32[]{:S(2)}) collective-permute-start(bf16[640,256]{1,0:T(8,128)(2,1)S(1)} %hand_on.5.refs_0_.refs_2_), channel_id=1, source_target_pairs={{0,8},{8,0},{16,24},{24,16},{32,40},{40,32},{48,56},{56,48},{64,72... | collective-permute-start | bytes 983048 | tf_op jit(solution)/shard_map/ppermute | solution.py:380
  32.5 13.4 %collective-permute-start.4 = (bf16[640,256]{1,0:T(8,128)(2,1)S(1)}, bf16[640,256]{1,0:T(8,128)(2,1)S(1)}, u32[]{:S(2)}, u32[]{:S(2)}) collective-permute-start(bf16[640,256]{1,0:T(8,128)(2,1)S(1)} %hand_on.4), channel_id=1, source_target_pairs={{0,8},{8,0},{16,24},{24,16},{32,40},{40,32},{48,56},{56,48},{64,72... | collective-permute-start | bytes 983048 | tf_op jit(solution)/shard_map/ppermute | solution.py:378
  33.1 12.6 %collective-permute-start.9 = (bf16[640,256]{1,0:T(8,128)(2,1)S(1)}, bf16[640,256]{1,0:T(8,128)(2,1)S(1)}, u32[]{:S(2)}, u32[]{:S(2)}) collective-permute-start(bf16[640,256]{1,0:T(8,128)(2,1)S(1)} %hand_on.5.refs_0_.refs_2_), channel_id=1, source_target_pairs={{32,64},{40,72},{48,80},{56,88},{64,96},{72,104},{80,112},{88,120}... | collective-permute-start | bytes 983048 | tf_op jit(solution)/shard_map/ppermute | solution.py:379
  45.7 3.9 %collective-permute-start.10 = (bf16[640,256]{1,0:T(8,128)(2,1)S(1)}, bf16[640,256]{1,0:T(8,128)(2,1)S(1)}, u32[]{:S(2)}, u32[]{:S(2)}) collective-permute-start(bf16[640,256]{1,0:T(8,128)(2,1)S(1)} %hand_on.7.refs_6_), channel_id=1, source_target_pairs={{0,8},{8,0},{16,24},{24,16},{32,40},{40,32},{48,56},{56,48},{64,72... | collective-permute-start | bytes 983048 | tf_op jit(solution)/shard_map/ppermute | solution.py:384
